TPU v7x, 256 devices: a whole 4x4x8 slice. The times are simulated.
256 devices in a mesh: cell: 32 (over x, z), wall: 8 (over y, core).
Axes of the slice: x: 4, y: 4, z: 8, core: 2. Of those that a mesh axis runs over, the one named last changes fastest.
Arguments:
- self_matrix: bfloat16 [64, 8, 1152, 1152], P('cell', 'wall'), may hold values from -0.1875 to 0.1875
- cell_source: float32 [64, 8, 3, 384], P('cell', 'wall'), may hold values from -6 to 6
- cell_pos: float32 [64, 8, 3, 384], P('cell', 'wall'), may hold values from -68 to 772, as said below
- wall_source: float32 [3, 1024, 6144], P(None, 'cell', 'wall'), may hold values from -6 to 6
- wall_coef: float32 [1024, 6144], P('cell', 'wall'), may hold values from 0.3 to 1.5
- pair_target: int32 [8, 256], P('wall'), may hold values from 0 to 63, as said below
- pair_source: int32 [8, 256], P('wall'), may hold values from 0 to 63, as said below
- pair_count: int32 [8, 32], P('wall'), may hold values from 1 to 8, as said below
- near_wall: int32 [64, 8, 1024], P('cell', 'wall'), may hold values from 0 to 51199, as said below
Outputs:
- cell_density: float32 [64, 8, 3, 384], P('cell', 'wall')
- wall_density: float32 [3, 1024, 6144], P(None, 'cell', 'wall')
Inputs may be any that keep to these rules, and one draw needn't show every extreme that they name: `cell_pos`: positions of the cells' points: each cell lies about one unit inside the wall above its owner's patch. `near_wall`: each cell's list is the 32 x 2 * 16 block of its device's patch with band (rows of 800 panels) around the cell's place over the wall, in row order. `pair_target`: every slot of device o names a cell of device o. `pair_source`: every slot's source cell lies on one of the two devices next to its owner along the cell axis, around the loop. `pair_count`: in every wall index one device has all 8 slots live.
All inputs are finite; a program needn't handle non-finite values.
Results may differ from a plain program's by a relative error of at most 0.00034.
Values sent between devices are 32-bit elements; how exact they have to be, the bound alone decides.
A program may use at most 128 MiB of HBM per device.

v0:
```python
import functools
import math

import jax
import jax.numpy as jnp
from jax import lax
from jax.experimental import pallas as pl
from jax.experimental.pallas import tpu as pltpu
from jax.sharding import PartitionSpec as P

REACH = 16
PAIR_CAP = 8
LANES = 128
ROWS = 8
BLOCK = 2 * REACH
KINDS = 16

panel_step = 0.125
smooth_eps2 = 0.25
panel_weight = 0.015625

MESH = pl.DeviceIdType.MESH
MINOR = (((1,), (1,)), ((), ()))
PLAIN = (((1,), (0,)), ((), ()))

AROUND = ((-1, 0), (1, 0), (0, -1), (0, 1), (-1, -1), (-1, 1), (1, -1), (1, 1))
F32 = jnp.float32
BF16 = jnp.bfloat16


def span(step, low, mid, high):
    return low if step < 0 else (high if step > 0 else mid)


def halves(value):
    high = value.astype(BF16)
    return high, (value - high.astype(F32)).astype(BF16)


def source_kinds(place, load):
    along = place[0] * load[0] + place[1] * load[1] + place[2] * load[2]
    norm = place[0] * place[0] + place[1] * place[1] + place[2] * place[2]
    kinds = [load[0], load[1], load[2]]
    for c in range(3):
        for i in range(3):
            kinds.append(2.0 * load[c] * place[i] + load[i] * place[c])
    for c in range(3):
        kinds.append(along * place[c] + norm * load[c])
    return kinds


def target_sum(place, sums):
    norm = place[0] * place[0] + place[1] * place[1] + place[2] * place[2]
    along = place[0] * sums[0] + place[1] * sums[1] + place[2] * sums[2]
    trace = (sums[3] + sums[7] + sums[11]) * (1.0 / 3.0)
    out = []
    for c in range(3):
        cross = place[0] * sums[3 + 3 * c] + place[1] * sums[4 + 3 * c] + place[2] * sums[5 + 3 * c]
        out.append(
            (norm + 2.0 * smooth_eps2) * sums[c] + place[c] * (along - trace) - cross + sums[12 + c]
        )
    return out


def body(
    n_cell,
    n_wall,
    near_ref,
    target_ref,
    source_ref,
    count_ref,
    matrix_hbm,
    cell_hbm,
    pos_hbm,
    wall_hbm,
    coef_hbm,
    cell_out,
    wall_out,
    matrix,
    own_pos,
    dens,
    near_pos,
    near_dens,
    coef,
    wall_ext0,
    wall_ext1,
    spill,
    from_rows,
    from_cols,
    from_corners,
    centred,
    columns,
    places,
    level,
    kinds_f32,
    kinds,
    flat_kinds,
    wall_sums,
    local_sem,
    small_send,
    small_recv,
    dens_send,
    dens_recv,
    wall_send,
    wall_recv,
    spill_send,
    spill_recv,
):
    wall_ext = (wall_ext0, wall_ext1)
    cells, _, points = own_pos.shape
    span_theta, span_axial = coef.shape
    ext_axial = span_axial + 2 * REACH
    theta_total = span_theta * n_cell
    point_tiles = points // LANES
    wall_tiles = BLOCK * BLOCK // LANES
    tiles = wall_tiles + 2 * cells * point_tiles
    pair_scale = 8.0 / points
    ext_tiles = span_axial // LANES + 2
    ext_groups = (span_theta + 2 * REACH) // ROWS
    row_groups = span_theta // ROWS + 1
    me_cell = lax.axis_index("cell")
    me_wall = lax.axis_index("wall")

    def device(step):
        return (
            lax.rem(me_cell + step[0] + n_cell, n_cell),
            lax.rem(me_wall + step[1] + n_wall, n_wall),
        )

    locals_ = []
    for number, (src, dst) in enumerate(
        [
            (pos_hbm.at[:, 0], own_pos),
            (cell_hbm.at[:, 0], dens.at[0]),
            (wall_hbm, wall_ext[0].at[:, pl.ds(REACH, span_theta), pl.ds(LANES, span_axial)]),
            (coef_hbm, coef),
        ]
        + [(matrix_hbm.at[k, 0], matrix.at[k]) for k in range(cells)]
    ):
        copy = pltpu.make_async_copy(src, dst, local_sem.at[number])
        copy.start()
        locals_.append(copy)

    barrier = pltpu.get_barrier_semaphore()
    for step in AROUND:
        pl.semaphore_signal(barrier, inc=1, device_id=device(step), device_id_type=MESH)
    pl.semaphore_wait(barrier, len(AROUND))

    def remote(src, dst, send, recv, step):
        copy = pltpu.make_async_remote_copy(
            src_ref=src, dst_ref=dst, send_sem=send, recv_sem=recv,
            device_id=device(step), device_id_type=MESH,
        )
        copy.start()
        return copy

    small = []
    for side, step in enumerate(((1, 0), (-1, 0))):
        small.append(
            remote(pos_hbm.at[:, 0], near_pos.at[side], small_send.at[0, side], small_recv.at[0, side], step)
        )
        small.append(
            remote(cell_hbm.at[:, 0], near_dens.at[0, side], small_send.at[1, side], small_recv.at[1, side], step)
        )

    def send_band(src, row_base, lane_base, which):
        out = []
        for number, step in enumerate(AROUND):
            rows = span(step[0], REACH, span_theta, REACH)
            lanes = span(step[1], LANES, span_axial, LANES)
            from_row = row_base + span(step[0], 0, 0, span_theta - REACH)
            from_lane = lane_base + span(step[1], 0, 0, span_axial - LANES)
            to_row = span(step[0], REACH + span_theta, REACH, 0)
            to_lane = span(step[1], LANES + span_axial, LANES, 0)
            out.append(
                remote(
                    src.at[:, pl.ds(from_row, rows), pl.ds(from_lane, lanes)],
                    wall_ext[which].at[:, pl.ds(to_row, rows), pl.ds(to_lane, lanes)],
                    wall_send.at[which, number],
                    wall_recv.at[which, number],
                    step,
                )
            )
        return out

    band = [send_band(wall_hbm, 0, 0, 0), None]

    lane_iota = lax.broadcasted_iota(jnp.int32, (ROWS, LANES), 1)
    row_iota = lax.broadcasted_iota(jnp.int32, (ROWS, LANES), 0)
    in_block = lane_iota % BLOCK
    block_row = row_iota + ROWS * (lane_iota // BLOCK)

    row_shift, row_group, offset, held_tile, held_chunk, theta_of, axial_of = [], [], [], [], [], [], []
    for k in range(cells):
        first = jnp.broadcast_to(near_ref[k, :, 0:1], (ROWS, LANES))
        row = ((first.astype(F32) + 0.5) * (1.0 / ext_axial)).astype(jnp.int32)
        column = first - row * ext_axial
        lane = column + (LANES - REACH)
        off = lane & (LANES - 1)
        row_shift.append(row & (ROWS - 1))
        row_group.append(row >> 3)
        offset.append(off)
        held_tile.append((lane >> 7) + jnp.where(lane_iota < off, 1, 0))
        held_chunk.append(((lane_iota - off) & (LANES - 1)) >> 5)
        theta_of.append(me_cell * span_theta - REACH + row + block_row)
        axial_of.append(me_wall * span_axial - REACH + column + in_block)

    def turn_lanes(value, amount):
        for bit in range(7):
            value = jnp.where((amount & (1 << bit)) != 0, pltpu.roll(value, 1 << bit, axis=1), value)
        return value

    def turn_rows(value, amount):
        for bit in range(3):
            value = jnp.where((amount & (1 << bit)) != 0, pltpu.roll(value, 1 << bit, axis=0), value)
        return value

    locals_[0].wait()
    locals_[1].wait()

    centre = []
    for k in range(cells):
        mid = jnp.sum(own_pos[k], axis=1, keepdims=True) * (1.0 / points)
        centre.append(mid)
        rel = own_pos[k] - mid
        centred[k] = rel
        for c in range(3):
            for j in range(point_tiles):
                piece = jnp.broadcast_to(rel[c : c + 1, j * LANES : (j + 1) * LANES], (LANES, LANES))
                columns[k, c, pl.ds(j * LANES, LANES), :] = piece.T
        theta = theta_of[k].astype(F32)
        axial = axial_of[k].astype(F32)
        angle = (2.0 * math.pi / theta_total) * theta
        radius = theta_total * panel_step / (2.0 * math.pi)
        places[k, 0, pl.ds(0, ROWS), :] = radius * jnp.cos(angle) - mid[0:1]
        places[k, 1, pl.ds(0, ROWS), :] = radius * jnp.sin(angle) - mid[1:2]
        places[k, 2, pl.ds(0, ROWS), :] = panel_step * axial - mid[2:3]

    def fill_level(k, first, last):
        def one(tile, carry):
            y = [
                jnp.broadcast_to(places[k, c, pl.ds(tile, 1), :], (BLOCK // 2, LANES))
                for c in range(3)
            ]
            lanes = pl.ds(pl.multiple_of(tile * LANES, LANES), LANES)
            for g in range(points // 16):
                rows = pl.ds(16 * g, 16)
                dx = columns[k, 0, rows, :] - y[0]
                dy = columns[k, 1, rows, :] - y[1]
                dz = columns[k, 2, rows, :] - y[2]
                inverse = lax.rsqrt(dx * dx + dy * dy + dz * dz + smooth_eps2)
                high, low = halves(inverse * inverse * inverse)
                level[k, rows, lanes] = high
                level[k, pl.ds(points + 16 * g, 16), lanes] = low
            return carry

        lax.fori_loop(first, last, one, 0)

    for k in range(cells):
        fill_level(k, 0, wall_tiles)

    def to_wall(turn):
        blocks = []
        for k in range(cells):
            rel = centred[k]
            load = dens[turn, k] * pair_scale
            rows = source_kinds(
                [rel[c : c + 1] for c in range(3)], [load[c : c + 1] for c in range(3)]
            )
            rows.append(jnp.zeros_like(rows[0]))
            high, low = halves(jnp.concatenate(rows, axis=0))
            flat_kinds[pl.ds(0, KINDS), pl.ds(0, points)] = high
            flat_kinds[pl.ds(0, KINDS), pl.ds(points, points)] = high
            flat_kinds[pl.ds(KINDS, KINDS), pl.ds(0, points)] = low
            flat_kinds[pl.ds(KINDS, KINDS), pl.ds(points, points)] = low
            sums = lax.dot_general(
                flat_kinds[...], level[k, :, pl.ds(0, wall_tiles * LANES)], PLAIN,
                preferred_element_type=F32,
            )
            sums = sums[:KINDS] + sums[KINDS:]
            for a in range(wall_tiles):
                wall_sums[k, pl.ds(a * KINDS, KINDS), :] = sums[:, a * LANES : (a + 1) * LANES]
            by_kind = [wall_sums[k, pl.ds(n, wall_tiles, stride=KINDS), :] for n in range(15)]
            place = [places[k, c, pl.ds(0, ROWS), :] for c in range(3)]
            found = target_sum(place, by_kind)
            shift, group = row_shift[k], row_group[k]
            laid = []
            for c in range(3):
                turned = turn_rows(turn_lanes(found[c], offset[k]), shift)
                parts = [
                    jnp.where(held_chunk[k] == 0, pltpu.roll(turned, LANES - BLOCK * b, axis=1) if b else turned, 0.0)
                    for b in range(BLOCK // ROWS)
                ]
                steps = []
                for j in range(BLOCK // ROWS + 1):
                    low = parts[j] if j < len(parts) else jnp.zeros_like(turned)
                    high = parts[j - 1] if j > 0 else jnp.zeros_like(turned)
                    steps.append(jnp.where(row_iota >= shift, low, high))
                rows_ = []
                for g in range(ext_groups):
                    value = jnp.zeros_like(turned)
                    for r in range(row_groups):
                        if 0 <= g - r < len(steps):
                            value = jnp.where(group == r, steps[g - r], value)
                    rows_.append(value)
                laid.append(rows_)
            blocks.append(laid)
        for t in range(ext_tiles):
            here = [held_tile[k] == t for k in range(cells)]
            for c in range(3):
                for g in range(ext_groups):
                    total = jnp.where(here[0], blocks[0][c][g], 0.0)
                    for k in range(1, cells):
                        total = total + jnp.where(here[k], blocks[k][c][g], 0.0)
                    spill[turn, c, pl.ds(ROWS * g, ROWS), pl.ds(t * LANES, LANES)] = total
        out = []
        for number, step in enumerate(AROUND):
            rows = span(step[0], REACH, span_theta, REACH)
            lanes = span(step[1], LANES, span_axial, LANES)
            from_row = span(step[0], 0, REACH, REACH + span_theta)
            from_lane = span(step[1], 0, LANES, LANES + span_axial)
            if step[1] == 0:
                dst = from_rows.at[turn, number]
            elif step[0] == 0:
                dst = from_cols.at[turn, number - 2]
            else:
                dst = from_corners.at[turn, number - 4]
            out.append(
                remote(
                    spill.at[turn, :, pl.ds(from_row, rows), pl.ds(from_lane, lanes)],
                    dst,
                    spill_send.at[turn, number],
                    spill_recv.at[turn, number],
                    step,
                )
            )
        return out

    spills = [to_wall(0), None]

    def self_term(turn, k):
        flat = jnp.concatenate([dens[turn, k, c : c + 1] for c in range(3)], axis=1)
        rows = jnp.broadcast_to(flat, (16, flat.shape[1])).astype(BF16)
        found = lax.dot_general(rows, matrix[k], MINOR, preferred_element_type=F32)
        return jnp.concatenate([found[0:1, c * points : (c + 1) * points] for c in range(3)], axis=0)

    for k in range(cells):
        locals_[4 + k].wait()
    velocity = [self_term(0, k) for k in range(cells)]

    slots = target_ref.shape[1]
    slot = lax.broadcasted_iota(jnp.int32, (1, slots), 1)
    device_lane = lax.broadcasted_iota(jnp.int32, count_ref.shape, 1)
    live = jnp.sum(jnp.where(device_lane == me_cell, count_ref[...], 0).astype(F32), axis=1, keepdims=True)
    first_slot = me_cell * PAIR_CAP
    in_use = (slot >= first_slot) & ((slot - first_slot).astype(F32) < live)
    sides = (lax.rem(me_cell + n_cell - 1, n_cell), lax.rem(me_cell + 1, n_cell))
    weight = []
    for k in range(cells):
        mine = in_use & (target_ref[...] == me_cell * cells + k)
        weight.append(
            [
                jnp.sum(
                    jnp.where(mine & (source_ref[...] == sides[s // cells] * cells + s % cells), pair_scale, 0.0),
                    axis=1,
                    keepdims=True,
                )
                for s in range(2 * cells)
            ]
        )

    for copy in small:
        copy.wait_recv()
    for k in range(cells):
        for s in range(2 * cells):
            rel = near_pos[s // cells, s % cells] - centre[k]
            for c in range(3):
                for j in range(point_tiles):
                    places[k, c, pl.ds(wall_tiles + s * point_tiles + j, 1), :] = rel[
                        c : c + 1, j * LANES : (j + 1) * LANES
                    ]
    for k in range(cells):
        fill_level(k, wall_tiles, tiles)

    def stencil(which):
        found = []
        for c in range(3):
            mid = wall_ext[which][c, pl.ds(REACH, span_theta), :]
            width = mid.shape[1]
            sides = pltpu.roll(mid, 1, axis=1) + pltpu.roll(mid, width - 1, axis=1)
            up = wall_ext[which][c, pl.ds(REACH + 1, span_theta), pl.ds(LANES, span_axial)]
            down = wall_ext[which][c, pl.ds(REACH - 1, span_theta), pl.ds(LANES, span_axial)]
            found.append(
                coef[...] * 0.25 * (up + down + sides[:, LANES : LANES + span_axial])
            )
        return found

    def wait_band(which):
        for copy in band[which]:
            copy.wait_recv()

    locals_[2].wait()
    locals_[3].wait()
    wait_band(0)
    first_wall = wall_ext[1].at[:, pl.ds(REACH, span_theta), pl.ds(LANES, span_axial)]
    found = stencil(0)
    for c in range(3):
        first_wall[c] = (
            wall_ext[0][c, pl.ds(REACH, span_theta), pl.ds(LANES, span_axial)]
            + found[c]
            + spill[0, c, pl.ds(REACH, span_theta), pl.ds(LANES, span_axial)]
        )
    for copy in spills[0]:
        copy.wait_recv()

    def add_fold(turn, out_ref):
        for number, step in enumerate(AROUND):
            rows = span(step[0], REACH, span_theta, REACH)
            lanes = span(step[1], LANES, span_axial, LANES)
            to_row = span(step[0], span_theta - REACH, 0, 0)
            to_lane = span(step[1], span_axial - LANES, 0, 0)
            if step[1] == 0:
                piece = from_rows[turn, number]
            elif step[0] == 0:
                piece = from_cols[turn, number - 2]
            else:
                piece = from_corners[turn, number - 4]
            view = out_ref.at[:, pl.ds(to_row, rows), pl.ds(to_lane, lanes)]
            view[...] = view[...] + piece

    add_fold(0, first_wall)
    band[1] = send_band(wall_ext[1], REACH, LANES, 1)

    def to_cell(turn, k):
        loads = []
        for c in range(3):
            rows_ = []
            for g in range(ext_groups):
                value = None
                for t in range(ext_tiles):
                    piece = wall_ext[turn][c, pl.ds(ROWS * g, ROWS), pl.ds(t * LANES, LANES)]
                    value = piece if t == 0 else jnp.where(held_tile[k] == t, piece, value)
                rows_.append(value)
            steps = []
            for j in range(BLOCK // ROWS + 1):
                value = rows_[j]
                for r in range(1, row_groups):
                    if j + r < ext_groups:
                        value = jnp.where(row_group[k] == r, rows_[j + r], value)
                steps.append(turn_rows(value, ROWS - row_shift[k]))
            packed = None
            for b in range(BLOCK // ROWS):
                part = jnp.where(row_iota + row_shift[k] < ROWS, steps[b], steps[b + 1])
                part = pltpu.roll(part, BLOCK * b, axis=1) if b else part
                packed = jnp.where(held_chunk[k] == b, part, packed) if b else part
            picked = turn_lanes(packed, LANES - offset[k])
            rest = []
            for s in range(2 * cells):
                for j in range(point_tiles):
                    rest.append(
                        near_dens[turn, s // cells, s % cells, c : c + 1, j * LANES : (j + 1) * LANES]
                        * weight[k][s]
                    )
            rest += [jnp.zeros((1, LANES), F32)] * (places.shape[2] - tiles)
            loads.append(jnp.concatenate([picked * panel_weight] + rest, axis=0))
        place = [places[k, c] for c in range(3)]
        held = source_kinds(place, loads)
        for n in range(15):
            kinds_f32[pl.ds(n, places.shape[2], stride=KINDS), :] = held[n]
        for a in range(tiles):
            high, low = halves(kinds_f32[pl.ds(a * KINDS, KINDS), :])
            kinds[pl.ds(0, KINDS), pl.ds(a * LANES, LANES)] = high
            kinds[pl.ds(KINDS, KINDS), pl.ds(a * LANES, LANES)] = low
        sums = lax.dot_general(kinds[...], level[k], MINOR, preferred_element_type=F32)
        sums = sums[:KINDS] + sums[KINDS:]
        sums = sums[:, :points] + sums[:, points:]
        rel = centred[k]
        found = target_sum(
            [rel[c : c + 1] for c in range(3)], [sums[n : n + 1] for n in range(15)]
        )
        return jnp.concatenate(found, axis=0)

    kinds_f32[...] = jnp.zeros(kinds_f32.shape, F32)
    for k in range(cells):
        for c in range(3):
            places[k, c, pl.ds(tiles, places.shape[2] - tiles), :] = jnp.zeros(
                (places.shape[2] - tiles, LANES), F32
            )

    for k in range(cells):
        dens[1, k] = dens[0, k] + velocity[k] + to_cell(0, k)

    later = []
    for side, step in enumerate(((1, 0), (-1, 0))):
        later.append(
            remote(dens.at[1], near_dens.at[1, side], dens_send.at[side], dens_recv.at[side], step)
        )

    spills[1] = to_wall(1)
    velocity = [self_term(1, k) for k in range(cells)]

    wait_band(1)
    found = stencil(1)
    for c in range(3):
        wall_out[c] = (
            wall_ext[0][c, pl.ds(REACH, span_theta), pl.ds(LANES, span_axial)]
            + found[c]
            + spill[1, c, pl.ds(REACH, span_theta), pl.ds(LANES, span_axial)]
        )
    for copy in later:
        copy.wait_recv()
    for k in range(cells):
        cell_out[k, 0] = dens[0, k] + velocity[k] + to_cell(1, k)
    for copy in spills[1]:
        copy.wait_recv()
    add_fold(1, wall_out)

    for copy in small + band[0] + band[1] + spills[0] + spills[1] + later:
        copy.wait_send()


def local(
    n_cell, n_wall,
    self_matrix, cell_source, cell_pos, wall_source, wall_coef, pair_target, pair_source, pair_count, near_wall,
):
    cells, _, _, points = cell_pos.shape
    _, span_theta, span_axial = wall_source.shape
    unknowns = self_matrix.shape[-1]
    wall_tiles = BLOCK * BLOCK // LANES
    tiles = wall_tiles + 2 * cells * (points // LANES)
    rows = -(-tiles // ROWS) * ROWS
    ext_rows = span_theta + 2 * REACH
    ext_lanes = span_axial + 2 * LANES
    vmem = lambda *shape: pltpu.VMEM(shape, F32)
    dma = lambda *shape: pltpu.SemaphoreType.DMA(shape)
    hbm = pl.BlockSpec(memory_space=pl.ANY)
    full = pl.BlockSpec(memory_space=pltpu.VMEM)
    return pl.pallas_call(
        functools.partial(body, n_cell, n_wall),
        out_shape=(
            jax.ShapeDtypeStruct(cell_source.shape, F32),
            jax.ShapeDtypeStruct(wall_source.shape, F32),
        ),
        in_specs=[full] * 4 + [hbm] * 5,
        out_specs=(full, full),
        scratch_shapes=[
            pltpu.VMEM((cells, unknowns, unknowns), BF16),
            vmem(cells, 3, points),
            vmem(2, cells, 3, points),
            vmem(2, cells, 3, points),
            vmem(2, 2, cells, 3, points),
            vmem(span_theta, span_axial),
            vmem(3, ext_rows, ext_lanes),
            vmem(3, ext_rows, ext_lanes),
            vmem(2, 3, ext_rows, ext_lanes),
            vmem(2, 2, 3, REACH, span_axial),
            vmem(2, 2, 3, span_theta, LANES),
            vmem(2, 4, 3, REACH, LANES),
            vmem(cells, 3, points),
            vmem(cells, 3, points, LANES),
            vmem(cells, 3, rows, LANES),
            pltpu.VMEM((cells, 2 * points, tiles * LANES), BF16),
            vmem(rows * KINDS, LANES),
            pltpu.VMEM((2 * KINDS, tiles * LANES), BF16),
            pltpu.VMEM((2 * KINDS, 2 * points), BF16),
            vmem(cells, wall_tiles * KINDS, LANES),
            dma(4 + cells),
            dma(2, 2),
            dma(2, 2),
            dma(2),
            dma(2),
            dma(2, 8),
            dma(2, 8),
            dma(2, 8),
            dma(2, 8),
        ],
        compiler_params=pltpu.CompilerParams(
            collective_id=0, has_side_effects=True, vmem_limit_bytes=48 * 2**20
        ),
        cost_estimate=pl.CostEstimate(flops=2 * 10**9, bytes_accessed=8 * 10**6, transcendentals=2 * 10**6),
        name="picard",
    )(
        near_wall, pair_target, pair_source, pair_count,
        self_matrix, cell_source, cell_pos, wall_source, wall_coef,
    )


def solution(mesh):
    placed = (
        P("cell", "wall", None, None),
        P("cell", "wall", None, None),
        P("cell", "wall", None, None),
        P(None, "cell", "wall"),
        P("cell", "wall"),
        P("wall", None),
        P("wall", None),
        P("wall", None),
        P("cell", "wall", None),
    )
    return jax.shard_map(
        functools.partial(local, mesh.shape["cell"], mesh.shape["wall"]),
        mesh=mesh,
        in_specs=placed,
        out_specs=(P("cell", "wall", None, None), P(None, "cell", "wall")),
        check_vma=False,
    )
```

profile of v0, /device:TPU:1, one launch (start us, length us, event | category | flops | bytes accessed | tf_op | source)
XLA Modules:
  0.0 47.3 jit_solution(14472238034855297651)
XLA Ops:
  0.6 0.7 %copy.11.cell_hbm = f32[2,1,3,384]{3,2,1,0:T(4,128)S(1)} copy(f32[2,1,3,384]{3,1,2,0:T(1,128)} %param.10) | data formatting | bytes 18432 | tf_op args[1]
  1.3 0.7 %copy.12.pos_hbm = f32[2,1,3,384]{3,2,1,0:T(4,128)S(1)} copy(f32[2,1,3,384]{3,1,2,0:T(1,128)} %param.11) | data formatting | bytes 18432 | tf_op args[2]
  2.0 0.0 copy-start
  2.0 2.5 %copy-done = bf16[2,1,1152,1152]{3,2,1,0:T(8,128)(2,1)S(1)} copy-done((bf16[2,1,1152,1152]{3,2,1,0:T(8,128)(2,1)S(1)}, bf16[2,1,1152,1152]{3,2,1,0:T(8,128)(2,1)}, u32[]{:S(2)}) %copy-start) | copy-done | bytes 5308440
  4.5 0.0 copy-start.1
  4.5 1.0 %copy-done.1 = f32[3,32,768]{2,1,0:T(8,128)S(1)} copy-done((f32[3,32,768]{2,1,0:T(8,128)S(1)}, f32[3,32,768]{2,1,0:T(8,128)}, u32[]{:S(2)}) %copy-start.1) | copy-done | bytes 294936
  5.5 0.0 copy-start.2
  5.5 0.9 %copy-done.2 = f32[32,768]{1,0:T(8,128)S(1)} copy-done((f32[32,768]{1,0:T(8,128)S(1)}, f32[32,768]{1,0:T(8,128)}, u32[]{:S(2)}) %copy-start.2) | copy-done | bytes 98328
  6.4 0.0 copy-start.3
  6.4 0.7 %copy-done.3 = s32[2,1,1024]{2,1,0:T(1,128)S(1)} copy-done((s32[2,1,1024]{2,1,0:T(1,128)S(1)}, s32[2,1,1024]{2,1,0:T(1,128)}, u32[]{:S(2)}) %copy-start.3) | copy-done | bytes 8216
  7.1 0.0 copy-start.4
  7.1 0.7 %copy-done.4 = s32[1,256]{1,0:T(1,128)S(1)} copy-done((s32[1,256]{1,0:T(1,128)S(1)}, s32[1,256]{1,0:T(1,128)}, u32[]{:S(2)}) %copy-start.4) | copy-done | bytes 1048
  7.8 0.0 copy-start.5
  7.8 0.7 %copy-done.5 = s32[1,256]{1,0:T(1,128)S(1)} copy-done((s32[1,256]{1,0:T(1,128)S(1)}, s32[1,256]{1,0:T(1,128)}, u32[]{:S(2)}) %copy-start.5) | copy-done | bytes 1048
  8.5 0.0 copy-start.6
  8.5 0.7 %copy-done.6 = s32[1,32]{1,0:T(1,128)S(1)} copy-done((s32[1,32]{1,0:T(1,128)S(1)}, s32[1,32]{1,0:T(1,128)}, u32[]{:S(2)}) %copy-start.6) | copy-done | bytes 152
  9.1 36.9 %picard.1 = (f32[2,1,3,384]{3,2,1,0:T(4,128)S(1)}, f32[3,32,768]{2,1,0:T(8,128)S(1)}) custom-call(s32[2,1,1024]{2,1,0:T(1,128)S(1)} %copy-done.3, s32[1,256]{1,0:T(1,128)S(1)} %copy-done.4, s32[1,256]{1,0:T(1,128)S(1)} %copy-done.5, s32[1,32]{1,0:T(1,128)S(1)} %copy-done.6, bf16[2,1,1152,1152]{3,2,1,0:T(8,128)(2,1)S(1)} %copy-done, ...), custom_call_target="tpu_custom_call" | custom-call | flops 2000000000 | bytes 8000000 | tf_op jit(solution)/shard_map/picard/pallas_call | solution.py:538
  46.0 0.6 %copy.13 = f32[2,1,3,384]{3,1,2,0:T(1,128)} copy(f32[2,1,3,384]{3,2,1,0:T(4,128)S(1)} %get-tuple-element.2) | data formatting | bytes 18432 | tf_op jit(solution)/shard_map/picard/pallas_call | solution.py:538
  46.6 0.7 %copy.15 = f32[3,32,768]{2,1,0:T(8,128)} copy(f32[3,32,768]{2,1,0:T(8,128)S(1)} %get-tuple-element.7) | data formatting | bytes 589824
Async XLA Ops:
  2.0 2.5 %copy-start = (bf16[2,1,1152,1152]{3,2,1,0:T(8,128)(2,1)S(1)}, bf16[2,1,1152,1152]{3,2,1,0:T(8,128)(2,1)}, u32[]{:S(2)}) copy-start(bf16[2,1,1152,1152]{3,2,1,0:T(8,128)(2,1)} %matrix_hbm.1) | copy-start | bytes 15925252
  4.5 1.0 %copy-start.1 = (f32[3,32,768]{2,1,0:T(8,128)S(1)}, f32[3,32,768]{2,1,0:T(8,128)}, u32[]{:S(2)}) copy-start(f32[3,32,768]{2,1,0:T(8,128)} %wall_hbm.1) | copy-start | bytes 884740
  5.5 0.9 %copy-start.2 = (f32[32,768]{1,0:T(8,128)S(1)}, f32[32,768]{1,0:T(8,128)}, u32[]{:S(2)}) copy-start(f32[32,768]{1,0:T(8,128)} %coef_hbm.1) | copy-start | bytes 294916
  6.4 0.7 %copy-start.3 = (s32[2,1,1024]{2,1,0:T(1,128)S(1)}, s32[2,1,1024]{2,1,0:T(1,128)}, u32[]{:S(2)}) copy-start(s32[2,1,1024]{2,1,0:T(1,128)} %near_ref.1) | copy-start | bytes 24580
  7.1 0.7 %copy-start.4 = (s32[1,256]{1,0:T(1,128)S(1)}, s32[1,256]{1,0:T(1,128)}, u32[]{:S(2)}) copy-start(s32[1,256]{1,0:T(1,128)} %target_ref.1) | copy-start | bytes 3076
  7.8 0.7 %copy-start.5 = (s32[1,256]{1,0:T(1,128)S(1)}, s32[1,256]{1,0:T(1,128)}, u32[]{:S(2)}) copy-start(s32[1,256]{1,0:T(1,128)} %source_ref.1) | copy-start | bytes 3076
  8.5 0.7 %copy-start.6 = (s32[1,32]{1,0:T(1,128)S(1)}, s32[1,32]{1,0:T(1,128)}, u32[]{:S(2)}) copy-start(s32[1,32]{1,0:T(1,128)} %count_ref.1) | copy-start | bytes 388
where the time goes:
time: 47.7 us; the launch traced here: 47.3 us
  Pallas kernels  36.9 us (77%)
  local copies, waits for them, and re-layouts  9.8 us (21%)
  between operations  0.65 us (1%)
    pallas_call x1, Pallas kernels, local(): pl.pallas_call(functools.partial(body, n_cell, n_wall), out_shape=(jax.Sh...  36.9 us
    unnamed x17, local copies, waits for them, and re-layouts  9.19 us

commit v1 on v0

v1 whole, which is shorter than its diff:
```python
import functools
import math

import jax
import jax.numpy as jnp
from jax import lax
from jax.experimental import pallas as pl
from jax.experimental.pallas import tpu as pltpu
from jax.sharding import PartitionSpec as P

REACH = 16
PAIR_CAP = 8
LANES = 128
ROWS = 8
BLOCK = 2 * REACH
KINDS = 16

panel_step = 0.125
smooth_eps2 = 0.25
panel_weight = 0.015625

MESH = pl.DeviceIdType.MESH
MINOR = (((1,), (1,)), ((), ()))
PLAIN = (((1,), (0,)), ((), ()))

AROUND = ((-1, 0), (1, 0), (0, -1), (0, 1), (-1, -1), (-1, 1), (1, -1), (1, 1))
F32 = jnp.float32
BF16 = jnp.bfloat16


def span(step, low, mid, high):
    return low if step < 0 else (high if step > 0 else mid)


def halves(value):
    high = value.astype(BF16)
    return high, (value - high.astype(F32)).astype(BF16)


def source_kinds(place, load):
    along = place[0] * load[0] + place[1] * load[1] + place[2] * load[2]
    norm = place[0] * place[0] + place[1] * place[1] + place[2] * place[2]
    kinds = [load[0], load[1], load[2]]
    for c in range(3):
        for i in range(3):
            kinds.append(2.0 * load[c] * place[i] + load[i] * place[c])
    for c in range(3):
        kinds.append(along * place[c] + norm * load[c])
    return kinds


def target_sum(place, sums):
    norm = place[0] * place[0] + place[1] * place[1] + place[2] * place[2]
    along = place[0] * sums[0] + place[1] * sums[1] + place[2] * sums[2]
    trace = (sums[3] + sums[7] + sums[11]) * (1.0 / 3.0)
    out = []
    for c in range(3):
        cross = place[0] * sums[3 + 3 * c] + place[1] * sums[4 + 3 * c] + place[2] * sums[5 + 3 * c]
        out.append(
            (norm + 2.0 * smooth_eps2) * sums[c] + place[c] * (along - trace) - cross + sums[12 + c]
        )
    return out


def three(value):
    high = value.astype(BF16).astype(F32)
    rest = value - high
    mid = rest.astype(BF16).astype(F32)
    return high, mid, rest - mid


def square_sides(place, of_target):
    norm = place[0] * place[0] + place[1] * place[1] + place[2] * place[2]
    one = jnp.ones_like(norm)
    rows = []
    for c in range(3):
        high, mid, low = three(place[c] if of_target else -2.0 * place[c])
        rows += [high, high, mid, high, low, mid] if of_target else [high, mid, high, low, high, mid]
    if of_target:
        return rows + [*three(norm + smooth_eps2), one, one, one]
    return rows + [one, one, one, *three(norm)]


def body(
    n_cell,
    n_wall,
    near_hbm,
    target_hbm,
    source_hbm,
    count_hbm,
    matrix_hbm,
    cell_hbm,
    pos_hbm,
    wall_hbm,
    coef_hbm,
    cell_out,
    wall_out,
    matrix,
    state,
    near_state,
    dens1,
    near_dens1,
    coef,
    wall_ext0,
    wall_ext1,
    spill0,
    spill1,
    got_spill,
    pack,
    got_pack,
    near_own,
    near_got,
    target_row,
    source_row,
    count_row,
    columns,
    sources,
    places,
    level,
    square_f32,
    kinds_f32,
    kinds,
    flat_kinds,
    wall_sums,
    spread,
    gather,
    every,
    unturn,
    turn_spread,
    replica,
    held_groups,
    local_sem,
    state_send,
    state_recv,
    dens_send,
    dens_recv,
    near_send,
    near_recv,
    wall_send,
    wall_recv,
    edge_send,
    edge_recv,
    pack_send,
    pack_recv,
    spill_send,
    spill_recv,
):
    cells, points = matrix.shape[0], state.shape[-1]
    span_theta, span_axial = coef.shape
    ext_axial = span_axial + 2 * REACH
    theta_total = span_theta * n_cell
    point_tiles = points // LANES
    wall_tiles = BLOCK * BLOCK // LANES
    tiles = wall_tiles + 2 * cells * point_tiles
    tile_rows = places.shape[2]
    pair_scale = 8.0 / points
    own_tiles = span_axial // LANES
    ext_tiles = own_tiles + 2
    ext_groups = (span_theta + 2 * REACH) // ROWS
    row_groups = span_theta // ROWS + 1
    chunks = BLOCK // ROWS
    pairs_of_groups = ext_groups // 2
    spill = (spill0, spill1)
    me_cell = lax.axis_index("cell")
    me_wall = lax.axis_index("wall")

    def device(step):
        return (
            lax.rem(me_cell + step[0] + n_cell, n_cell),
            lax.rem(me_wall + step[1] + n_wall, n_wall),
        )

    own_near = near_hbm.at[:, :, pl.ds(0, LANES)]
    inside = []
    for number, (src, dst) in enumerate(
        [
            (pos_hbm, state.at[0]),
            (cell_hbm, state.at[1]),
            (own_near, near_own),
            (wall_hbm, wall_ext0.at[:, pl.ds(REACH, span_theta), pl.ds(LANES, span_axial)]),
            (coef_hbm, coef),
            (target_hbm, target_row),
            (source_hbm, source_row),
            (count_hbm, count_row),
        ]
        + [(matrix_hbm.at[k, 0], matrix.at[k]) for k in range(cells)]
    ):
        copy = pltpu.make_async_copy(src, dst, local_sem.at[number])
        copy.start()
        inside.append(copy)

    barrier = pltpu.get_barrier_semaphore()
    for step in AROUND:
        pl.semaphore_signal(barrier, inc=1, device_id=device(step), device_id_type=MESH)

    def remote(src, dst, send, recv, step):
        copy = pltpu.make_async_remote_copy(
            src_ref=src, dst_ref=dst, send_sem=send, recv_sem=recv,
            device_id=device(step), device_id_type=MESH,
        )
        copy.start()
        return copy

    lane_iota = lax.broadcasted_iota(jnp.int32, (ROWS, LANES), 1)
    row_iota = lax.broadcasted_iota(jnp.int32, (ROWS, LANES), 0)
    chunk_iota = lane_iota // BLOCK
    in_block = lane_iota % BLOCK
    block_row = row_iota + ROWS * chunk_iota
    nothing = jnp.zeros((ROWS, LANES), F32)

    in_chunk = lane_iota % BLOCK

    class Block:
        def __init__(self, first):
            first = jnp.broadcast_to(first, (ROWS, LANES))
            self.row = ((first.astype(F32) + 0.5) * (1.0 / ext_axial)).astype(jnp.int32)
            self.column = first - self.row * ext_axial
            lane = self.column + (LANES - REACH)
            self.turn = lane & (BLOCK - 1)
            self.shift = self.row & (ROWS - 1)
            self.group = self.row >> 3
            self.where = (lane >> 5) + jnp.where(in_chunk < self.turn, 1, 0) - chunk_iota

    def turn_rows(value, amount):
        for bit in range(3):
            value = jnp.where((amount & (1 << bit)) != 0, pltpu.roll(value, 1 << bit, axis=0), value)
        return value

    def moved(values, matrix_, dims=PLAIN):
        count = values.shape[0]
        terms = jnp.concatenate(three(values), axis=0).astype(BF16)
        out = lax.dot_general(terms, matrix_, dims, preferred_element_type=F32)
        return out[:count] + out[count : 2 * count] + out[2 * count :]

    def stacked(values):
        return jnp.concatenate(values, axis=0)

    def zero_one(mask):
        return jnp.where(mask, 1.0, 0.0).astype(BF16)

    from_lane = lax.broadcasted_iota(jnp.int32, (LANES, LANES), 0)
    to_lane_ = lax.broadcasted_iota(jnp.int32, (LANES, LANES), 1)
    same = (from_lane & (BLOCK - 1)) == (to_lane_ & (BLOCK - 1))
    every[...] = zero_one(same)
    for q in range(chunks):
        spread[:, pl.ds(q * LANES, LANES)] = zero_one(same & (from_lane >> 5 == q))
        gather[pl.ds(q * LANES, LANES), :] = zero_one(same & (to_lane_ >> 5 == q))

    square_f32[...] = jnp.zeros(square_f32.shape, F32)
    kinds_f32[...] = jnp.zeros(kinds_f32.shape, F32)
    sources[...] = jnp.zeros(sources.shape, BF16)

    inside[0].wait()
    inside[1].wait()
    inside[2].wait()
    own_block = [Block(near_own[k, :, 0:1]) for k in range(cells)]
    for k in range(cells):
        turn = jnp.broadcast_to(own_block[k].turn[0:1], (LANES, LANES))
        same = ((from_lane + turn) & (BLOCK - 1)) == (to_lane_ & (BLOCK - 1))
        unturn[k] = zero_one(same & (from_lane >> 5 == to_lane_ >> 5))
        for q in range(chunks):
            turn_spread[k, :, pl.ds(q * LANES, LANES)] = zero_one(same & (from_lane >> 5 == q))

    def rows_of(ref, k):
        return [ref[k, c] for c in range(3)]

    def fill_sources(k, first, count):
        place = [places[k, c, pl.ds(first, count), :] for c in range(3)]
        for n, value in enumerate(square_sides(place, False)):
            square_f32[pl.ds(first * BLOCK + n, count, stride=BLOCK), :] = value
        for a in range(first, min(first + count, tiles)):
            sources[k, pl.ds(0, BLOCK), pl.ds(a * LANES, LANES)] = square_f32[
                pl.ds(a * BLOCK, BLOCK), :
            ].astype(BF16)

    def fill_level(k, first, last):
        def one(step, carry):
            lanes = pl.ds(pl.multiple_of(step * 2 * LANES, 2 * LANES), 2 * LANES)
            square = lax.dot_general(columns[k], sources[k, :, lanes], PLAIN, preferred_element_type=F32)
            inverse = lax.rsqrt(square)
            high, low = halves(inverse * inverse * inverse)
            level[k, pl.ds(0, points), lanes] = high
            level[k, pl.ds(points, points), lanes] = low
            return carry

        lax.fori_loop(first // 2, last // 2, one, 0)

    centre, centred = [], []
    for k in range(cells):
        own = rows_of(state.at[0], k)
        mid = [jnp.sum(own[c], axis=1, keepdims=True) * (1.0 / points) for c in range(3)]
        rel = [own[c] - mid[c] for c in range(3)]
        centre.append(mid)
        centred.append(rel)
        rows = square_sides(rel, True)
        rows = jnp.concatenate(rows + [jnp.zeros((LANES - len(rows), points), F32)], axis=0)
        for j in range(point_tiles):
            columns[k, pl.ds(j * LANES, LANES), :] = rows[:, j * LANES : (j + 1) * LANES].T.astype(BF16)
        theta = (me_cell * span_theta - REACH + own_block[k].row + block_row).astype(F32)
        axial = (me_wall * span_axial - REACH + own_block[k].column + in_block).astype(F32)
        angle = (2.0 * math.pi / theta_total) * theta
        radius = theta_total * panel_step / (2.0 * math.pi)
        places[k, 0, pl.ds(0, ROWS), :] = radius * jnp.cos(angle) - mid[0]
        places[k, 1, pl.ds(0, ROWS), :] = radius * jnp.sin(angle) - mid[1]
        places[k, 2, pl.ds(0, ROWS), :] = panel_step * axial - mid[2]
        for c in range(3):
            places[k, c, pl.ds(tiles, tile_rows - tiles), :] = jnp.zeros((tile_rows - tiles, LANES), F32)
        fill_sources(k, 0, wall_tiles)
        fill_level(k, 0, wall_tiles)

    def to_wall(turn):
        merged = [[nothing] * 3 for _ in range(pairs_of_groups)]
        for k in range(cells):
            load = rows_of(state.at[1] if turn == 0 else dens1, k)
            rows = source_kinds(centred[k], [value * pair_scale for value in load])
            rows.append(jnp.zeros_like(rows[0]))
            high, low = halves(jnp.concatenate(rows, axis=0))
            flat_kinds[pl.ds(0, KINDS), pl.ds(0, points)] = high
            flat_kinds[pl.ds(0, KINDS), pl.ds(points, points)] = high
            flat_kinds[pl.ds(KINDS, KINDS), pl.ds(0, points)] = low
            flat_kinds[pl.ds(KINDS, KINDS), pl.ds(points, points)] = low
            sums = lax.dot_general(
                flat_kinds[...], level[k, :, pl.ds(0, wall_tiles * LANES)], PLAIN,
                preferred_element_type=F32,
            )
            sums = sums[:KINDS] + sums[KINDS:]
            for a in range(wall_tiles):
                wall_sums[k, pl.ds(a * KINDS, KINDS), :] = sums[:, a * LANES : (a + 1) * LANES]
            by_kind = [wall_sums[k, pl.ds(n, wall_tiles, stride=KINDS), :] for n in range(15)]
            found = target_sum([places[k, c, pl.ds(0, ROWS), :] for c in range(3)], by_kind)
            block = own_block[k]
            parts = moved(stacked([turn_rows(value, block.shift) for value in found]), turn_spread[k])
            for c in range(3):
                part = [
                    parts[c * ROWS : (c + 1) * ROWS, q * LANES : (q + 1) * LANES] for q in range(chunks)
                ]
                steps = [
                    jnp.where(
                        row_iota >= block.shift,
                        part[j] if j < chunks else nothing,
                        part[j - 1] if j else nothing,
                    )
                    for j in range(chunks + 1)
                ]
                for g in range(ext_groups):
                    value = nothing
                    for r in range(row_groups):
                        if 0 <= g - r <= chunks:
                            value = jnp.where(block.group == r, steps[g - r], value)
                    merged[g // 2][c] = jnp.where(chunk_iota == 2 * k + g % 2, value, merged[g // 2][c])
        for v in range(pairs_of_groups):
            for c in range(3):
                spill[turn][v, c] = merged[v][c]

    def cut_of(step):
        return span(step[0], (0, 1), (1, 2), (3, 1))

    def send_spill(turn):
        out = []
        for number, step in enumerate(AROUND):
            first, count = cut_of(step)
            out.append(
                remote(
                    spill[turn].at[pl.ds(first, count)],
                    got_spill.at[turn, number, pl.ds(0, count)],
                    spill_send.at[turn, number],
                    spill_recv.at[turn, number],
                    step,
                )
            )
        return out

    to_wall(0)
    pl.semaphore_wait(barrier, len(AROUND))

    beside = [
        remote(state, near_state.at[side], state_send.at[side], state_recv.at[side], step)
        for side, step in enumerate(((1, 0), (-1, 0)))
    ]
    band = []
    for number, step in enumerate(AROUND):
        rows = span(step[0], REACH, span_theta, REACH)
        lanes = span(step[1], LANES, span_axial, LANES)
        from_row = span(step[0], 0, 0, span_theta - REACH)
        from_lane = span(step[1], 0, 0, span_axial - LANES)
        to_row = span(step[0], REACH + span_theta, REACH, 0)
        to_lane = span(step[1], LANES + span_axial, LANES, 0)
        band.append(
            remote(
                wall_hbm.at[:, pl.ds(from_row, rows), pl.ds(from_lane, lanes)],
                wall_ext0.at[:, pl.ds(to_row, rows), pl.ds(to_lane, lanes)],
                wall_send.at[number],
                wall_recv.at[number],
                step,
            )
        )
    around = [
        remote(own_near, near_got.at[number], near_send.at[number], near_recv.at[number], step)
        for number, step in enumerate(AROUND)
    ]
    spills = [send_spill(0), None]

    def self_term(turn, k):
        flat = jnp.concatenate(rows_of(state.at[1] if turn == 0 else dens1, k), axis=1)
        rows = jnp.broadcast_to(flat, (16, flat.shape[1])).astype(BF16)
        found = lax.dot_general(rows, matrix[k], MINOR, preferred_element_type=F32)
        return [found[0:1, c * points : (c + 1) * points] for c in range(3)]

    for copy in inside[3:]:
        copy.wait()
    velocity = [self_term(0, k) for k in range(cells)]

    slots = target_row.shape[1]
    slot = lax.broadcasted_iota(jnp.int32, (1, slots), 1)
    device_lane = lax.broadcasted_iota(jnp.int32, count_row.shape, 1)
    live = jnp.sum(jnp.where(device_lane == me_cell, count_row[...], 0).astype(F32), axis=1, keepdims=True)
    first_slot = me_cell * PAIR_CAP
    in_use = (slot >= first_slot) & ((slot - first_slot).astype(F32) < live)
    sides = (lax.rem(me_cell + n_cell - 1, n_cell), lax.rem(me_cell + 1, n_cell))
    weight = []
    for k in range(cells):
        mine = in_use & (target_row[...] == me_cell * cells + k)
        weight.append(
            [
                jnp.sum(
                    jnp.where(mine & (source_row[...] == sides[s // cells] * cells + s % cells), pair_scale, 0.0),
                    axis=1,
                    keepdims=True,
                )
                for s in range(2 * cells)
            ]
        )

    for copy in beside:
        copy.wait_recv()
    for k in range(cells):
        for s in range(2 * cells):
            for c in range(3):
                rel = near_state[s // cells, 0, s % cells, c] - centre[k][c]
                for j in range(point_tiles):
                    places[k, c, pl.ds(wall_tiles + s * point_tiles + j, 1), :] = rel[
                        :, j * LANES : (j + 1) * LANES
                    ]
        fill_sources(k, wall_tiles, tile_rows - wall_tiles)
        fill_level(k, wall_tiles, tiles)

    def add_spill(turn, view):
        for half in range(2):
            origins = [(spill[turn], 1 + half, own_where, 0)]
            for number, step in enumerate(AROUND):
                if step[0] == 0:
                    origins.append((got_spill.at[turn, number], half, got_where[number], step[1]))
                elif (step[0] > 0) == (half == 0):
                    origins.append((got_spill.at[turn, number], 0, got_where[number], step[1]))
            replica[pl.ds(0, len(origins) * 3 * ROWS), :] = moved(
                stacked([ref[v, c] for ref, v, _, _ in origins for c in range(3)]), spread[...]
            )
            for t in range(own_tiles):
                sums = {}
                for o, (_, _, blocks, aside) in enumerate(origins):
                    if aside and t != (0 if aside > 0 else own_tiles - 1):
                        continue
                    for k in range(cells):
                        mask = blocks[k] == chunks * (t + 1 + own_tiles * aside)
                        for c in range(3):
                            for g in range(2):
                                part = replica[
                                    pl.ds((3 * o + c) * ROWS, ROWS), pl.ds((2 * k + g) * LANES, LANES)
                                ]
                                part = jnp.where(mask, part, 0.0)
                                sums[c, g] = sums[c, g] + part if (c, g) in sums else part
                for (c, g), value in sums.items():
                    spot = view.at[c, pl.ds(2 * ROWS * half + ROWS * g, ROWS), pl.ds(t * LANES, LANES)]
                    spot[...] = spot[...] + value

    def stencil(ref):
        found = []
        for c in range(3):
            mid = ref[c, pl.ds(REACH, span_theta), :]
            width = mid.shape[1]
            sides_ = pltpu.roll(mid, 1, axis=1) + pltpu.roll(mid, width - 1, axis=1)
            up = ref[c, pl.ds(REACH + 1, span_theta), pl.ds(LANES, span_axial)]
            down = ref[c, pl.ds(REACH - 1, span_theta), pl.ds(LANES, span_axial)]
            found.append(coef[...] * 0.25 * (up + down + sides_[:, LANES : LANES + span_axial]))
        return found

    def block_loads(groups, k):
        block = own_block[k]
        out = []
        for c in range(3):
            steps = []
            for j in range(chunks + 1):
                value = groups(c, j)
                for r in range(1, row_groups):
                    if j + r < ext_groups:
                        value = jnp.where(block.group == r, groups(c, j + r), value)
                steps.append(turn_rows(value, ROWS - block.shift))
            packed = nothing
            for b in range(chunks):
                part = jnp.where(row_iota + block.shift < ROWS, steps[b], steps[b + 1])
                packed = jnp.where(chunk_iota == b, part, packed)
            out.append(packed)
        out = moved(stacked(out), unturn[k], MINOR)
        return [out[c * ROWS : (c + 1) * ROWS] for c in range(3)]

    def to_cell(turn, k, picked):
        loads = []
        for c in range(3):
            rest = []
            for s in range(2 * cells):
                if turn == 0:
                    beside_load = near_state[s // cells, 1, s % cells, c]
                else:
                    beside_load = near_dens1[s // cells, s % cells, c]
                beside_load = beside_load * weight[k][s]
                for j in range(point_tiles):
                    rest.append(beside_load[:, j * LANES : (j + 1) * LANES])
            rest += [jnp.zeros((1, LANES), F32)] * (tile_rows - tiles)
            loads.append(jnp.concatenate([picked[c] * panel_weight] + rest, axis=0))
        held = source_kinds([places[k, c] for c in range(3)], loads)
        for n in range(15):
            kinds_f32[pl.ds(n, tile_rows, stride=KINDS), :] = held[n]
        for a in range(tiles):
            high, low = halves(kinds_f32[pl.ds(a * KINDS, KINDS), :])
            kinds[pl.ds(0, KINDS), pl.ds(a * LANES, LANES)] = high
            kinds[pl.ds(KINDS, KINDS), pl.ds(a * LANES, LANES)] = low
        sums = lax.dot_general(kinds[...], level[k], MINOR, preferred_element_type=F32)
        sums = sums[:KINDS] + sums[KINDS:]
        sums = sums[:, :points] + sums[:, points:]
        return target_sum(centred[k], [sums[n : n + 1] for n in range(15)])

    for copy in band:
        copy.wait_recv()
    centre_rows = pl.ds(REACH, span_theta)
    centre_lanes = pl.ds(LANES, span_axial)
    first_wall = wall_ext1.at[:, centre_rows, centre_lanes]
    found = stencil(wall_ext0)
    for c in range(3):
        first_wall[c] = wall_ext0[c, centre_rows, centre_lanes] + found[c]
    for copy in around + spills[0]:
        copy.wait_recv()
    got_where = [[Block(near_got[number, k, :, 0:1]).where for k in range(cells)] for number in range(len(AROUND))]
    own_where = [own_block[k].where for k in range(cells)]
    add_spill(0, first_wall)

    units = [(number, v, first) for number, step in enumerate(AROUND)
             for v, first in enumerate(span(step[0], (0,), (0, 2), (2,)))]
    units += [(None, 0, 0), (None, 1, 2)]
    for u, (number, v, first) in enumerate(units):
        step = (0, 0) if number is None else AROUND[number]
        blocks = own_where if number is None else got_where[AROUND.index((-step[0], -step[1]))]
        held = span(step[1], [0], range(own_tiles), [own_tiles - 1])
        for k in range(cells):
            masks = [(t, blocks[k] == chunks * (t + 1 - own_tiles * step[1])) for t in held]
            for c in range(3):
                for g in range(2):
                    rows = pl.ds(REACH + ROWS * (first + g), ROWS)
                    one = nothing
                    for t, mask in masks:
                        one = jnp.where(mask, wall_ext1[c, rows, pl.ds((t + 1) * LANES, LANES)], one)
                    replica[pl.ds((3 * u + c) * ROWS, ROWS), pl.ds((2 * k + g) * LANES, LANES)] = one
    packed = moved(replica[...], gather[...])
    for u, (number, v, first) in enumerate(units):
        for c in range(3):
            pack[len(AROUND) if number is None else number, v, c] = packed[(3 * u + c) * ROWS : (3 * u + c + 1) * ROWS]
    packs = []
    for number, step in enumerate(AROUND):
        count = 2 if step[0] == 0 else 1
        packs.append(
            remote(
                pack.at[number, pl.ds(0, count)],
                got_pack.at[number, pl.ds(0, count)],
                pack_send.at[number],
                pack_recv.at[number],
                step,
            )
        )

    def band_loads(k):
        masks = [own_where[k] == chunks * t for t in range(ext_tiles)]
        for c in range(3):
            for g in range(ext_groups):
                value = nothing
                for t in range(ext_tiles):
                    piece = wall_ext0[c, pl.ds(ROWS * g, ROWS), pl.ds(t * LANES, LANES)]
                    value = jnp.where(masks[t], piece, value)
                held_groups[pl.ds((c * ext_groups + g) * ROWS, ROWS), :] = value
        held_groups[...] = moved(held_groups[...], every[...])
        return block_loads(lambda c, g: held_groups[pl.ds((c * ext_groups + g) * ROWS, ROWS), :], k)

    for k in range(cells):
        found = to_cell(0, k, band_loads(k))
        for c in range(3):
            dens1[k, c] = state[1, k, c] + velocity[k][c] + found[c]

    later = [
        remote(dens1, near_dens1.at[side], dens_send.at[side], dens_recv.at[side], step)
        for side, step in enumerate(((1, 0), (-1, 0)))
    ]
    to_wall(1)
    spills[1] = send_spill(1)

    edge = []
    for number, step in enumerate(AROUND[:4]):
        rows = span(step[0], ROWS, span_theta, ROWS)
        lanes = span(step[1], LANES, span_axial, LANES)
        from_row = REACH + span(step[0], 0, 0, span_theta - ROWS)
        from_lane = LANES + span(step[1], 0, 0, span_axial - LANES)
        to_row = span(step[0], REACH + span_theta, REACH, REACH - ROWS)
        to_lane = span(step[1], LANES + span_axial, LANES, 0)
        edge.append(
            remote(
                wall_ext1.at[:, pl.ds(from_row, rows), pl.ds(from_lane, lanes)],
                wall_ext1.at[:, pl.ds(to_row, rows), pl.ds(to_lane, lanes)],
                edge_send.at[number],
                edge_recv.at[number],
                step,
            )
        )

    velocity = [self_term(1, k) for k in range(cells)]

    for copy in packs:
        copy.wait_recv()
    cut = [[nothing] * 3 for _ in range(pairs_of_groups)]
    for v in range(2):
        for c in range(3):
            cut[1 + v][c] = pack[len(AROUND), v, c]
    for number, step in enumerate(AROUND):
        first, count = span(step[0], (3, 1), (1, 2), (0, 1))
        for v in range(count):
            for c in range(3):
                cut[first + v][c] = cut[first + v][c] + got_pack[number, v, c]
    cut_rows = 3 * pairs_of_groups * ROWS
    replica[pl.ds(0, cut_rows), :] = moved(stacked([value for per in cut for value in per]), spread[...])

    def pack_loads(k):
        return block_loads(
            lambda c, g: replica[
                pl.ds((g // 2 * 3 + c) * ROWS, ROWS), pl.ds((2 * k + g % 2) * LANES, LANES)
            ],
            k,
        )

    for copy in later:
        copy.wait_recv()
    for k in range(cells):
        found = to_cell(1, k, pack_loads(k))
        for c in range(3):
            cell_out[k, c] = state[1, k, c] + velocity[k][c] + found[c]

    for copy in edge:
        copy.wait_recv()
    found = stencil(wall_ext1)
    for c in range(3):
        wall_out[c] = wall_ext0[c, centre_rows, centre_lanes] + found[c]
    for copy in spills[1]:
        copy.wait_recv()
    add_spill(1, wall_out)

    for copy in beside + band + around + spills[0] + packs + later + spills[1] + edge:
        copy.wait_send()


def local(
    n_cell, n_wall,
    self_matrix, cell_source, cell_pos, wall_source, wall_coef, pair_target, pair_source, pair_count, near_wall,
):
    cells, _, _, points = cell_pos.shape
    _, span_theta, span_axial = wall_source.shape
    unknowns = self_matrix.shape[-1]
    wall_tiles = BLOCK * BLOCK // LANES
    tiles = wall_tiles + 2 * cells * (points // LANES)
    rows = -(-tiles // ROWS) * ROWS
    ext_rows = span_theta + 2 * REACH
    ext_lanes = span_axial + 2 * LANES
    vmem = lambda *shape: pltpu.VMEM(shape, F32)
    ints = lambda *shape: pltpu.VMEM(shape, jnp.int32)
    dma = lambda *shape: pltpu.SemaphoreType.DMA(shape)
    hbm = pl.BlockSpec(memory_space=pl.ANY)
    full = pl.BlockSpec(memory_space=pltpu.VMEM)
    by_component = (cells, 3, 1, points)
    velocity, wall = pl.pallas_call(
        functools.partial(body, n_cell, n_wall),
        out_shape=(
            jax.ShapeDtypeStruct(by_component, F32),
            jax.ShapeDtypeStruct(wall_source.shape, F32),
        ),
        in_specs=[hbm] * 9,
        out_specs=(full, full),
        scratch_shapes=[
            pltpu.VMEM((cells, unknowns, unknowns), BF16),
            vmem(2, *by_component),
            vmem(2, 2, *by_component),
            vmem(*by_component),
            vmem(2, *by_component),
            vmem(span_theta, span_axial),
            vmem(3, ext_rows, ext_lanes),
            vmem(3, ext_rows, ext_lanes),
            vmem(4, 3, ROWS, LANES),
            vmem(4, 3, ROWS, LANES),
            vmem(2, 8, 2, 3, ROWS, LANES),
            vmem(9, 2, 3, ROWS, LANES),
            vmem(8, 2, 3, ROWS, LANES),
            ints(cells, 1, LANES),
            ints(8, cells, 1, LANES),
            ints(*pair_target.shape),
            ints(*pair_source.shape),
            ints(*pair_count.shape),
            pltpu.VMEM((cells, points, LANES), BF16),
            pltpu.VMEM((cells, LANES, tiles * LANES), BF16),
            vmem(cells, 3, rows, LANES),
            pltpu.VMEM((cells, 2 * points, tiles * LANES), BF16),
            vmem(rows * BLOCK, LANES),
            vmem(rows * KINDS, LANES),
            pltpu.VMEM((2 * KINDS, tiles * LANES), BF16),
            pltpu.VMEM((2 * KINDS, 2 * points), BF16),
            vmem(cells, wall_tiles * KINDS, LANES),
            pltpu.VMEM((LANES, 4 * LANES), BF16),
            pltpu.VMEM((4 * LANES, LANES), BF16),
            pltpu.VMEM((LANES, LANES), BF16),
            pltpu.VMEM((cells, LANES, LANES), BF16),
            pltpu.VMEM((cells, LANES, 4 * LANES), BF16),
            vmem(12 * 3 * ROWS, 4 * LANES),
            vmem(3 * ext_rows, LANES),
            dma(8 + cells),
            dma(2),
            dma(2),
            dma(2),
            dma(2),
            dma(8),
            dma(8),
            dma(8),
            dma(8),
            dma(4),
            dma(4),
            dma(8),
            dma(8),
            dma(2, 8),
            dma(2, 8),
        ],
        compiler_params=pltpu.CompilerParams(
            collective_id=0, has_side_effects=True, vmem_limit_bytes=60 * 2**20
        ),
        cost_estimate=pl.CostEstimate(flops=2 * 10**9, bytes_accessed=8 * 10**6, transcendentals=2 * 10**6),
        name="picard",
    )(
        near_wall, pair_target, pair_source, pair_count,
        self_matrix, cell_source.transpose(0, 2, 1, 3), cell_pos.transpose(0, 2, 1, 3), wall_source, wall_coef,
    )
    return velocity.transpose(0, 2, 1, 3), wall


def solution(mesh):
    placed = (
        P("cell", "wall", None, None),
        P("cell", "wall", None, None),
        P("cell", "wall", None, None),
        P(None, "cell", "wall"),
        P("cell", "wall"),
        P("wall", None),
        P("wall", None),
        P("wall", None),
        P("cell", "wall", None),
    )
    return jax.shard_map(
        functools.partial(local, mesh.shape["cell"], mesh.shape["wall"]),
        mesh=mesh,
        in_specs=placed,
        out_specs=(P("cell", "wall", None, None), P(None, "cell", "wall")),
        check_vma=False,
    )
```

time: 47.7 us -> 36.9 us (0.77)
  local copies, waits for them, and re-layouts: 9.8 us -> 3 us
  Pallas kernels: 36.9 us -> 33 us
    unnamed x17 -> x2, local copies, waits for them, and re-layouts: 9.19 us -> 3 us
    pallas_call x1, Pallas kernels: 36.9 us -> 33 us  [local(): pl.pallas_call(functools.partial(body, n_cell, n_wall), out_shape=(jax.Sh...]
    pallas_call x1 -> x0, local copies, waits for them, and re-layouts: 0.61 us -> none  [local(): pl.pallas_call(functools.partial(body, n_cell, n_wall), out_shape=(jax.Sh...]
where the time goes in v1:
time: 36.9 us; the launch traced here: 36.6 us
  Pallas kernels  33 us (89%)
  local copies, waits for them, and re-layouts  3 us (8%)
  between operations  0.64 us (2%)
    pallas_call x1, Pallas kernels, local(): pl.pallas_call(functools.partial(body, n_cell, n_wall), out_shape=(jax.Sh...  33 us
    unnamed x2, local copies, waits for them, and re-layouts  3 us

profile of v1, /device:TPU:1, one launch (start us, length us, event | category | flops | bytes accessed | tf_op | source)
XLA Modules:
  0.0 36.6 jit_solution(4005565398861335485)
XLA Ops:
  0.6 33.0 %picard.1 = (f32[2,3,1,384]{3,2,1,0:T(1,128)}, f32[3,32,768]{2,1,0:T(8,128)}) custom-call(s32[2,1,1024]{2,1,0:T(1,128)} %near_hbm.1, s32[1,256]{1,0:T(1,128)} %target_hbm.1, s32[1,256]{1,0:T(1,128)} %source_hbm.1, s32[1,32]{1,0:T(1,128)} %count_hbm.1, bf16[2,1,1152,1152]{3,2,1,0:T(8,128)(2,1)} %matrix_hbm.1, f32[2,3,1,384]{3,2,1,0:T(1,128)} %bitcast.4, ...), custom_call_target="tpu_custom_call" | custom-call | flops 2000000000 | bytes 8000000 | tf_op jit(solution)/shard_map/picard/pallas_call | solution.py:683
  33.6 1.3 %copy.13 = f32[2,1,3,384]{3,1,2,0:T(1,128)} copy(f32[2,1,3,384]{3,1,2,0:T(1,128)} %bitcast.3) | data formatting | bytes 18432
  34.9 1.7 %copy.14 = f32[3,32,768]{2,1,0:T(8,128)} copy(f32[3,32,768]{2,1,0:T(8,128)} %get-tuple-element.9) | data formatting | bytes 589824

commit v2 on v1

--- a/solution.py
+++ b/solution.py
@@ -105,11 +105,11 @@
     wall_ext1,
     spill0,
     spill1,
-    got_spill,
+    got_spill0,
+    got_spill1,
     pack,
     got_pack,
     near_own,
-    near_got,
     target_row,
     source_row,
     count_row,
@@ -134,8 +134,6 @@
     state_recv,
     dens_send,
     dens_recv,
-    near_send,
-    near_recv,
     wall_send,
     wall_recv,
     edge_send,
@@ -160,7 +158,7 @@
     row_groups = span_theta // ROWS + 1
     chunks = BLOCK // ROWS
     pairs_of_groups = ext_groups // 2
-    spill = (spill0, spill1)
+    spill, got_spill = (spill0, spill1), (got_spill0, got_spill1)
     me_cell = lax.axis_index("cell")
     me_wall = lax.axis_index("wall")
 
@@ -169,6 +167,10 @@
             lax.rem(me_cell + step[0] + n_cell, n_cell),
             lax.rem(me_wall + step[1] + n_wall, n_wall),
         )
+
+    barrier = pltpu.get_barrier_semaphore()
+    for step in AROUND:
+        pl.semaphore_signal(barrier, inc=1, device_id=device(step), device_id_type=MESH)
 
     own_near = near_hbm.at[:, :, pl.ds(0, LANES)]
     inside = []
@@ -189,10 +191,6 @@
         copy.start()
         inside.append(copy)
 
-    barrier = pltpu.get_barrier_semaphore()
-    for step in AROUND:
-        pl.semaphore_signal(barrier, inc=1, device_id=device(step), device_id_type=MESH)
-
     def remote(src, dst, send, recv, step):
         copy = pltpu.make_async_remote_copy(
             src_ref=src, dst_ref=dst, send_sem=send, recv_sem=recv,
@@ -214,7 +212,7 @@
         def __init__(self, first):
             first = jnp.broadcast_to(first, (ROWS, LANES))
             self.row = ((first.astype(F32) + 0.5) * (1.0 / ext_axial)).astype(jnp.int32)
-            self.column = first - self.row * ext_axial
+            self.column = first.astype(jnp.int32) - self.row * ext_axial
             lane = self.column + (LANES - REACH)
             self.turn = lane & (BLOCK - 1)
             self.shift = self.row & (ROWS - 1)
@@ -248,12 +246,15 @@
 
     square_f32[...] = jnp.zeros(square_f32.shape, F32)
     kinds_f32[...] = jnp.zeros(kinds_f32.shape, F32)
-    sources[...] = jnp.zeros(sources.shape, BF16)
 
     inside[0].wait()
     inside[1].wait()
     inside[2].wait()
     own_block = [Block(near_own[k, :, 0:1]) for k in range(cells)]
+    width = LANES // cells
+    own_first = nothing
+    for k in range(cells):
+        own_first = jnp.where(lane_iota // width == k, near_own[k, :, 0:1].astype(F32), own_first)
     for k in range(cells):
         turn = jnp.broadcast_to(own_block[k].turn[0:1], (LANES, LANES))
         same = ((from_lane + turn) & (BLOCK - 1)) == (to_lane_ & (BLOCK - 1))
@@ -269,21 +270,21 @@
         for n, value in enumerate(square_sides(place, False)):
             square_f32[pl.ds(first * BLOCK + n, count, stride=BLOCK), :] = value
         for a in range(first, min(first + count, tiles)):
-            sources[k, pl.ds(0, BLOCK), pl.ds(a * LANES, LANES)] = square_f32[
+            sources[k, :, pl.ds(a * LANES, LANES)] = square_f32[
                 pl.ds(a * BLOCK, BLOCK), :
             ].astype(BF16)
 
     def fill_level(k, first, last):
         def one(step, carry):
             lanes = pl.ds(pl.multiple_of(step * 2 * LANES, 2 * LANES), 2 * LANES)
-            square = lax.dot_general(columns[k], sources[k, :, lanes], PLAIN, preferred_element_type=F32)
+            square = lax.dot_general(columns[k, :, pl.ds(0, BLOCK)], sources[k, :, lanes], PLAIN, preferred_element_type=F32)
             inverse = lax.rsqrt(square)
             high, low = halves(inverse * inverse * inverse)
             level[k, pl.ds(0, points), lanes] = high
             level[k, pl.ds(points, points), lanes] = low
             return carry
 
-        lax.fori_loop(first // 2, last // 2, one, 0)
+        lax.fori_loop(first // 2, last // 2, one, 0, unroll=True)
 
     centre, centred = [], []
     for k in range(cells):
@@ -351,6 +352,8 @@
         for v in range(pairs_of_groups):
             for c in range(3):
                 spill[turn][v, c] = merged[v][c]
+            if turn == 0:
+                spill[turn][v, 3] = own_first
 
     def cut_of(step):
         return span(step[0], (0, 1), (1, 2), (3, 1))
@@ -362,7 +365,7 @@
             out.append(
                 remote(
                     spill[turn].at[pl.ds(first, count)],
-                    got_spill.at[turn, number, pl.ds(0, count)],
+                    got_spill[turn].at[number, pl.ds(0, count)],
                     spill_send.at[turn, number],
                     spill_recv.at[turn, number],
                     step,
@@ -377,6 +380,7 @@
         remote(state, near_state.at[side], state_send.at[side], state_recv.at[side], step)
         for side, step in enumerate(((1, 0), (-1, 0)))
     ]
+    spills = [send_spill(0), None]
     band = []
     for number, step in enumerate(AROUND):
         rows = span(step[0], REACH, span_theta, REACH)
@@ -394,11 +398,6 @@
                 step,
             )
         )
-    around = [
-        remote(own_near, near_got.at[number], near_send.at[number], near_recv.at[number], step)
-        for number, step in enumerate(AROUND)
-    ]
-    spills = [send_spill(0), None]
 
     def self_term(turn, k):
         flat = jnp.concatenate(rows_of(state.at[1] if turn == 0 else dens1, k), axis=1)
@@ -449,9 +448,9 @@
             origins = [(spill[turn], 1 + half, own_where, 0)]
             for number, step in enumerate(AROUND):
                 if step[0] == 0:
-                    origins.append((got_spill.at[turn, number], half, got_where[number], step[1]))
+                    origins.append((got_spill[turn].at[number], half, got_where[number], step[1]))
                 elif (step[0] > 0) == (half == 0):
-                    origins.append((got_spill.at[turn, number], 0, got_where[number], step[1]))
+                    origins.append((got_spill[turn].at[number], 0, got_where[number], step[1]))
             replica[pl.ds(0, len(origins) * 3 * ROWS), :] = moved(
                 stacked([ref[v, c] for ref, v, _, _ in origins for c in range(3)]), spread[...]
             )
@@ -503,7 +502,21 @@
         out = moved(stacked(out), unturn[k], MINOR)
         return [out[c * ROWS : (c + 1) * ROWS] for c in range(3)]
 
-    def to_cell(turn, k, picked):
+    def cell_sums(k, first, last, loads):
+        count = loads[0].shape[0]
+        held = source_kinds([places[k, c, pl.ds(first, count), :] for c in range(3)], loads)
+        for n in range(15):
+            kinds_f32[pl.ds(first * KINDS + n, count, stride=KINDS), :] = held[n]
+        for a in range(first, last):
+            high, low = halves(kinds_f32[pl.ds(a * KINDS, KINDS), :])
+            kinds[pl.ds(0, KINDS), pl.ds(a * LANES, LANES)] = high
+            kinds[pl.ds(KINDS, KINDS), pl.ds(a * LANES, LANES)] = low
+        lanes = pl.ds(first * LANES, (last - first) * LANES)
+        sums = lax.dot_general(kinds[:, lanes], level[k, :, lanes], MINOR, preferred_element_type=F32)
+        sums = sums[:KINDS] + sums[KINDS:]
+        return sums[:, :points] + sums[:, points:]
+
+    def pair_sums(turn, k):
         loads = []
         for c in range(3):
             rest = []
@@ -516,18 +529,16 @@
                 for j in range(point_tiles):
                     rest.append(beside_load[:, j * LANES : (j + 1) * LANES])
             rest += [jnp.zeros((1, LANES), F32)] * (tile_rows - tiles)
-            loads.append(jnp.concatenate([picked[c] * panel_weight] + rest, axis=0))
-        held = source_kinds([places[k, c] for c in range(3)], loads)
-        for n in range(15):
-            kinds_f32[pl.ds(n, tile_rows, stride=KINDS), :] = held[n]
-        for a in range(tiles):
-            high, low = halves(kinds_f32[pl.ds(a * KINDS, KINDS), :])
-            kinds[pl.ds(0, KINDS), pl.ds(a * LANES, LANES)] = high
-            kinds[pl.ds(KINDS, KINDS), pl.ds(a * LANES, LANES)] = low
-        sums = lax.dot_general(kinds[...], level[k], MINOR, preferred_element_type=F32)
-        sums = sums[:KINDS] + sums[KINDS:]
-        sums = sums[:, :points] + sums[:, points:]
+            loads.append(jnp.concatenate(rest, axis=0))
+        return cell_sums(k, wall_tiles, tiles, loads)
+
+    def near_sums(k, picked):
+        return cell_sums(k, 0, wall_tiles, [value * panel_weight for value in picked])
+
+    def to_cell(k, sums):
         return target_sum(centred[k], [sums[n : n + 1] for n in range(15)])
+
+    from_pairs = [pair_sums(0, k) for k in range(cells)]
 
     for copy in band:
         copy.wait_recv()
@@ -537,32 +548,40 @@
     found = stencil(wall_ext0)
     for c in range(3):
         first_wall[c] = wall_ext0[c, centre_rows, centre_lanes] + found[c]
-    for copy in around + spills[0]:
+    for copy in spills[0]:
         copy.wait_recv()
-    got_where = [[Block(near_got[number, k, :, 0:1]).where for k in range(cells)] for number in range(len(AROUND))]
+    got_where = [
+        [Block(got_spill0[number, 0, 3, 0:1, k * width : k * width + 1]).where for k in range(cells)]
+        for number in range(len(AROUND))
+    ]
     own_where = [own_block[k].where for k in range(cells)]
     add_spill(0, first_wall)
 
     units = [(number, v, first) for number, step in enumerate(AROUND)
              for v, first in enumerate(span(step[0], (0,), (0, 2), (2,)))]
-    units += [(None, 0, 0), (None, 1, 2)]
-    for u, (number, v, first) in enumerate(units):
-        step = (0, 0) if number is None else AROUND[number]
-        blocks = own_where if number is None else got_where[AROUND.index((-step[0], -step[1]))]
-        held = span(step[1], [0], range(own_tiles), [own_tiles - 1])
-        for k in range(cells):
-            masks = [(t, blocks[k] == chunks * (t + 1 - own_tiles * step[1])) for t in held]
+    own_units = [(None, 0, 0), (None, 1, 2)]
+
+    def make_packs(units, base):
+        for u, (number, v, first) in enumerate(units):
+            step = (0, 0) if number is None else AROUND[number]
+            blocks = own_where if number is None else got_where[AROUND.index((-step[0], -step[1]))]
+            held = span(step[1], [0], range(own_tiles), [own_tiles - 1])
+            for k in range(cells):
+                masks = [(t, blocks[k] == chunks * (t + 1 - own_tiles * step[1])) for t in held]
+                for c in range(3):
+                    for g in range(2):
+                        rows = pl.ds(REACH + ROWS * (first + g), ROWS)
+                        one = nothing
+                        for t, mask in masks:
+                            one = jnp.where(mask, wall_ext1[c, rows, pl.ds((t + 1) * LANES, LANES)], one)
+                        replica[pl.ds(base + (3 * u + c) * ROWS, ROWS), pl.ds((2 * k + g) * LANES, LANES)] = one
+        packed = moved(replica[pl.ds(base, 3 * ROWS * len(units)), :], gather[...])
+        for u, (number, v, first) in enumerate(units):
             for c in range(3):
-                for g in range(2):
-                    rows = pl.ds(REACH + ROWS * (first + g), ROWS)
-                    one = nothing
-                    for t, mask in masks:
-                        one = jnp.where(mask, wall_ext1[c, rows, pl.ds((t + 1) * LANES, LANES)], one)
-                    replica[pl.ds((3 * u + c) * ROWS, ROWS), pl.ds((2 * k + g) * LANES, LANES)] = one
-    packed = moved(replica[...], gather[...])
-    for u, (number, v, first) in enumerate(units):
-        for c in range(3):
-            pack[len(AROUND) if number is None else number, v, c] = packed[(3 * u + c) * ROWS : (3 * u + c + 1) * ROWS]
+                spot = len(AROUND) if number is None else number
+                pack[spot, v, c] = packed[(3 * u + c) * ROWS : (3 * u + c + 1) * ROWS]
+
+    make_packs(units, 0)
     packs = []
     for number, step in enumerate(AROUND):
         count = 2 if step[0] == 0 else 1
@@ -589,7 +608,7 @@
         return block_loads(lambda c, g: held_groups[pl.ds((c * ext_groups + g) * ROWS, ROWS), :], k)
 
     for k in range(cells):
-        found = to_cell(0, k, band_loads(k))
+        found = to_cell(k, from_pairs[k] + near_sums(k, band_loads(k)))
         for c in range(3):
             dens1[k, c] = state[1, k, c] + velocity[k][c] + found[c]
 
@@ -618,6 +637,7 @@
             )
         )
 
+    make_packs(own_units, 3 * ROWS * len(units))
     velocity = [self_term(1, k) for k in range(cells)]
 
     for copy in packs:
@@ -642,10 +662,11 @@
             k,
         )
 
+    from_wall = [near_sums(k, pack_loads(k)) for k in range(cells)]
     for copy in later:
         copy.wait_recv()
     for k in range(cells):
-        found = to_cell(1, k, pack_loads(k))
+        found = to_cell(k, pair_sums(1, k) + from_wall[k])
         for c in range(3):
             cell_out[k, c] = state[1, k, c] + velocity[k][c] + found[c]
 
@@ -658,7 +679,7 @@
         copy.wait_recv()
     add_spill(1, wall_out)
 
-    for copy in beside + band + around + spills[0] + packs + later + spills[1] + edge:
+    for copy in beside + band + spills[0] + packs + later + spills[1] + edge:
         copy.wait_send()
 
 
@@ -683,8 +704,8 @@
     velocity, wall = pl.pallas_call(
         functools.partial(body, n_cell, n_wall),
         out_shape=(
-            jax.ShapeDtypeStruct(by_component, F32),
-            jax.ShapeDtypeStruct(wall_source.shape, F32),
+            pltpu.VMEM(by_component, F32),
+            pltpu.VMEM(wall_source.shape, F32),
         ),
         in_specs=[hbm] * 9,
         out_specs=(full, full),
@@ -697,18 +718,18 @@
             vmem(span_theta, span_axial),
             vmem(3, ext_rows, ext_lanes),
             vmem(3, ext_rows, ext_lanes),
+            vmem(4, 4, ROWS, LANES),
             vmem(4, 3, ROWS, LANES),
-            vmem(4, 3, ROWS, LANES),
-            vmem(2, 8, 2, 3, ROWS, LANES),
+            vmem(8, 2, 4, ROWS, LANES),
+            vmem(8, 2, 3, ROWS, LANES),
             vmem(9, 2, 3, ROWS, LANES),
             vmem(8, 2, 3, ROWS, LANES),
             ints(cells, 1, LANES),
-            ints(8, cells, 1, LANES),
             ints(*pair_target.shape),
             ints(*pair_source.shape),
             ints(*pair_count.shape),
             pltpu.VMEM((cells, points, LANES), BF16),
-            pltpu.VMEM((cells, LANES, tiles * LANES), BF16),
+            pltpu.VMEM((cells, BLOCK, tiles * LANES), BF16),
             vmem(cells, 3, rows, LANES),
             pltpu.VMEM((cells, 2 * points, tiles * LANES), BF16),
             vmem(rows * BLOCK, LANES),
@@ -730,8 +751,6 @@
             dma(2),
             dma(8),
             dma(8),
-            dma(8),
-            dma(8),
             dma(4),
             dma(4),
             dma(8),

time: 36.9 us -> 33 us (0.89)
  Pallas kernels: 33 us -> 30.9 us
  local copies, waits for them, and re-layouts: 3 us -> 1.31 us
    pallas_call x1, Pallas kernels: 33 us -> 30.9 us  [local(): pl.pallas_call(functools.partial(body, n_cell, n_wall), out_shape=(pltpu....]
    unnamed x2, local copies, waits for them, and re-layouts: 3 us -> 1.31 us
where the time goes in v2:
time: 33 us; the launch traced here: 32.9 us
  Pallas kernels  30.9 us (94%)
  local copies, waits for them, and re-layouts  1.31 us (4%)
  between operations  0.64 us (2%)
    pallas_call x1, Pallas kernels, local(): pl.pallas_call(functools.partial(body, n_cell, n_wall), out_shape=(pltpu....  30.9 us
    unnamed x2, local copies, waits for them, and re-layouts  1.31 us

profile of v2, /device:TPU:1, one launch (start us, length us, event | category | flops | bytes accessed | tf_op | source)
XLA Modules:
  0.0 32.9 jit_solution(9276408344670048127)
XLA Ops:
  0.6 30.9 %picard.1 = (f32[2,3,1,384]{3,2,1,0:T(1,128)S(1)}, f32[3,32,768]{2,1,0:T(8,128)S(1)}) custom-call(s32[2,1,1024]{2,1,0:T(1,128)} %near_hbm.1, s32[1,256]{1,0:T(1,128)} %target_hbm.1, s32[1,256]{1,0:T(1,128)} %source_hbm.1, s32[1,32]{1,0:T(1,128)} %count_hbm.1, bf16[2,1,1152,1152]{3,2,1,0:T(8,128)(2,1)} %matrix_hbm.1, f32[2,3,1,384]{3,2,1,0:T(1,128)} %bitcast.4, ...), custom_call_target="tpu_custom_call" | custom-call | flops 2000000000 | bytes 8000000 | tf_op jit(solution)/shard_map/picard/pallas_call | solution.py:704
  31.6 0.6 %copy.13 = f32[2,1,3,384]{3,1,2,0:T(1,128)} copy(f32[2,1,3,384]{3,1,2,0:T(1,128)S(1)} %bitcast.3) | data formatting | bytes 18432
  32.2 0.7 %copy.14 = f32[3,32,768]{2,1,0:T(8,128)} copy(f32[3,32,768]{2,1,0:T(8,128)S(1)} %get-tuple-element.7) | data formatting | bytes 589824

commit v3 on v2

--- a/solution.py
+++ b/solution.py
@@ -109,6 +109,10 @@
     got_spill1,
     pack,
     got_pack,
+    own_edge,
+    got_edge,
+    own_corner,
+    got_corner,
     near_own,
     target_row,
     source_row,
@@ -138,6 +142,8 @@
     wall_recv,
     edge_send,
     edge_recv,
+    corner_send,
+    corner_recv,
     pack_send,
     pack_recv,
     spill_send,
@@ -374,15 +380,54 @@
         return out
 
     to_wall(0)
+    own_rows = pl.ds(REACH, span_theta)
+    own_lanes = pl.ds(LANES, span_axial)
+
+    def stage_edge(turn, ref):
+        for c in range(3):
+            own_edge[turn, 0, c] = ref[c, pl.ds(REACH, 1), own_lanes]
+            own_edge[turn, 1, c] = ref[c, pl.ds(REACH + span_theta - 1, 1), own_lanes]
+
+    def send_edge(turn):
+        return [
+            remote(
+                own_edge.at[turn, number], got_edge.at[turn, number],
+                edge_send.at[turn, number], edge_recv.at[turn, number], AROUND[number],
+            )
+            for number in range(2)
+        ]
+
+    corner_parts = [(g, c) for g in range(2) for c in range(3)]
+    inside[3].wait()
+    stage_edge(0, wall_ext0)
+    for number, step in enumerate(AROUND[4:]):
+        start = span(step[1], 0, 0, LANES - REACH)
+        tile = span(step[1], 1, 1, own_tiles)
+        value = nothing
+        for i, (g, c) in enumerate(corner_parts):
+            row = REACH + span(step[0], 0, 0, span_theta - REACH) + ROWS * g
+            part = wall_ext0[c, pl.ds(row, ROWS), pl.ds(tile * LANES, LANES)]
+            amount = (REACH * i - start) % LANES
+            part = pltpu.roll(part, amount, axis=1) if amount else part
+            value = jnp.where(lane_iota // REACH == i, part, value)
+        own_corner[number] = value
     pl.semaphore_wait(barrier, len(AROUND))
 
     beside = [
         remote(state, near_state.at[side], state_send.at[side], state_recv.at[side], step)
         for side, step in enumerate(((1, 0), (-1, 0)))
     ]
+    edges = [send_edge(0), None]
     spills = [send_spill(0), None]
+    corners = [
+        remote(
+            own_corner.at[number], got_corner.at[number],
+            corner_send.at[number], corner_recv.at[number], step,
+        )
+        for number, step in enumerate(AROUND[4:])
+    ]
     band = []
-    for number, step in enumerate(AROUND):
+    for number, step in enumerate(AROUND[:4]):
         rows = span(step[0], REACH, span_theta, REACH)
         lanes = span(step[1], LANES, span_axial, LANES)
         from_row = span(step[0], 0, 0, span_theta - REACH)
@@ -405,7 +450,7 @@
         found = lax.dot_general(rows, matrix[k], MINOR, preferred_element_type=F32)
         return [found[0:1, c * points : (c + 1) * points] for c in range(3)]
 
-    for copy in inside[3:]:
+    for copy in inside[4:]:
         copy.wait()
     velocity = [self_term(0, k) for k in range(cells)]
 
@@ -472,14 +517,16 @@
                     spot = view.at[c, pl.ds(2 * ROWS * half + ROWS * g, ROWS), pl.ds(t * LANES, LANES)]
                     spot[...] = spot[...] + value
 
-    def stencil(ref):
+    def stencil(ref, turn):
         found = []
+        rows = lax.broadcasted_iota(jnp.int32, (span_theta, span_axial), 0)
         for c in range(3):
-            mid = ref[c, pl.ds(REACH, span_theta), :]
-            width = mid.shape[1]
-            sides_ = pltpu.roll(mid, 1, axis=1) + pltpu.roll(mid, width - 1, axis=1)
-            up = ref[c, pl.ds(REACH + 1, span_theta), pl.ds(LANES, span_axial)]
-            down = ref[c, pl.ds(REACH - 1, span_theta), pl.ds(LANES, span_axial)]
+            wide = ref[c, own_rows, :]
+            width_ = wide.shape[1]
+            sides_ = pltpu.roll(wide, 1, axis=1) + pltpu.roll(wide, width_ - 1, axis=1)
+            mid = ref[c, own_rows, own_lanes]
+            up = jnp.where(rows == span_theta - 1, got_edge[turn, 0, c], pltpu.roll(mid, span_theta - 1, axis=0))
+            down = jnp.where(rows == 0, got_edge[turn, 1, c], pltpu.roll(mid, 1, axis=0))
             found.append(coef[...] * 0.25 * (up + down + sides_[:, LANES : LANES + span_axial]))
         return found
 
@@ -540,14 +587,9 @@
 
     from_pairs = [pair_sums(0, k) for k in range(cells)]
 
-    for copy in band:
-        copy.wait_recv()
-    centre_rows = pl.ds(REACH, span_theta)
-    centre_lanes = pl.ds(LANES, span_axial)
-    first_wall = wall_ext1.at[:, centre_rows, centre_lanes]
-    found = stencil(wall_ext0)
+    first_wall = wall_ext1.at[:, own_rows, own_lanes]
     for c in range(3):
-        first_wall[c] = wall_ext0[c, centre_rows, centre_lanes] + found[c]
+        first_wall[c] = wall_ext0[c, own_rows, own_lanes]
     for copy in spills[0]:
         copy.wait_recv()
     got_where = [
@@ -556,6 +598,12 @@
     ]
     own_where = [own_block[k].where for k in range(cells)]
     add_spill(0, first_wall)
+    for copy in edges[0] + band[2:]:
+        copy.wait_recv()
+    found = stencil(wall_ext0, 0)
+    for c in range(3):
+        first_wall[c] = first_wall[c] + found[c]
+    stage_edge(1, wall_ext1)
 
     units = [(number, v, first) for number, step in enumerate(AROUND)
              for v, first in enumerate(span(step[0], (0,), (0, 2), (2,)))]
@@ -607,6 +655,17 @@
         held_groups[...] = moved(held_groups[...], every[...])
         return block_loads(lambda c, g: held_groups[pl.ds((c * ext_groups + g) * ROWS, ROWS), :], k)
 
+    for copy in band[:2] + corners:
+        copy.wait_recv()
+    for number, step in enumerate(AROUND[4:]):
+        start = span(step[1], 0, 0, LANES - REACH)
+        tile = span(step[1], ext_tiles - 1, 0, 0)
+        for i, (g, c) in enumerate(corner_parts):
+            row = span(step[0], REACH + span_theta, 0, 0) + ROWS * g
+            amount = (start - REACH * i) % LANES
+            part = got_corner[number]
+            part = pltpu.roll(part, amount, axis=1) if amount else part
+            wall_ext0[c, pl.ds(row, ROWS), pl.ds(tile * LANES, LANES)] = part
     for k in range(cells):
         found = to_cell(k, from_pairs[k] + near_sums(k, band_loads(k)))
         for c in range(3):
@@ -619,20 +678,16 @@
     to_wall(1)
     spills[1] = send_spill(1)
 
-    edge = []
-    for number, step in enumerate(AROUND[:4]):
-        rows = span(step[0], ROWS, span_theta, ROWS)
-        lanes = span(step[1], LANES, span_axial, LANES)
-        from_row = REACH + span(step[0], 0, 0, span_theta - ROWS)
+    edges[1] = send_edge(1)
+    for number, step in enumerate(AROUND[2:4]):
         from_lane = LANES + span(step[1], 0, 0, span_axial - LANES)
-        to_row = span(step[0], REACH + span_theta, REACH, REACH - ROWS)
         to_lane = span(step[1], LANES + span_axial, LANES, 0)
-        edge.append(
+        edges[1].append(
             remote(
-                wall_ext1.at[:, pl.ds(from_row, rows), pl.ds(from_lane, lanes)],
-                wall_ext1.at[:, pl.ds(to_row, rows), pl.ds(to_lane, lanes)],
-                edge_send.at[number],
-                edge_recv.at[number],
+                wall_ext1.at[:, own_rows, pl.ds(from_lane, LANES)],
+                wall_ext1.at[:, own_rows, pl.ds(to_lane, LANES)],
+                edge_send.at[1, 2 + number],
+                edge_recv.at[1, 2 + number],
                 step,
             )
         )
@@ -670,16 +725,16 @@
         for c in range(3):
             cell_out[k, c] = state[1, k, c] + velocity[k][c] + found[c]
 
-    for copy in edge:
+    for copy in edges[1]:
         copy.wait_recv()
-    found = stencil(wall_ext1)
+    found = stencil(wall_ext1, 1)
     for c in range(3):
-        wall_out[c] = wall_ext0[c, centre_rows, centre_lanes] + found[c]
+        wall_out[c] = wall_ext0[c, own_rows, own_lanes] + found[c]
     for copy in spills[1]:
         copy.wait_recv()
     add_spill(1, wall_out)
 
-    for copy in beside + band + spills[0] + packs + later + spills[1] + edge:
+    for copy in beside + band + spills[0] + packs + later + spills[1] + edges[0] + edges[1] + corners:
         copy.wait_send()
 
 
@@ -724,6 +779,10 @@
             vmem(8, 2, 3, ROWS, LANES),
             vmem(9, 2, 3, ROWS, LANES),
             vmem(8, 2, 3, ROWS, LANES),
+            vmem(2, 2, 3, 1, span_axial),
+            vmem(2, 2, 3, 1, span_axial),
+            vmem(4, ROWS, LANES),
+            vmem(4, ROWS, LANES),
             ints(cells, 1, LANES),
             ints(*pair_target.shape),
             ints(*pair_source.shape),
@@ -749,8 +808,10 @@
             dma(2),
             dma(2),
             dma(2),
-            dma(8),
-            dma(8),
+            dma(4),
+            dma(4),
+            dma(2, 4),
+            dma(2, 4),
             dma(4),
             dma(4),
             dma(8),

time: 33 us -> 30.6 us (0.927)
  Pallas kernels: 30.9 us -> 28.5 us
    pallas_call x1, Pallas kernels: 30.9 us -> 28.5 us  [local(): pl.pallas_call(functools.partial(body, n_cell, n_wall), out_shape=(pltpu....]
where the time goes in v3:
time: 30.6 us; the launch traced here: 30.5 us
  Pallas kernels  28.5 us (93%)
  local copies, waits for them, and re-layouts  1.31 us (4%)
  between operations  0.64 us (2%)
    pallas_call x1, Pallas kernels, local(): pl.pallas_call(functools.partial(body, n_cell, n_wall), out_shape=(pltpu....  28.5 us
    unnamed x2, local copies, waits for them, and re-layouts  1.31 us

profile of v3, /device:TPU:1, one launch (start us, length us, event | category | flops | bytes accessed | tf_op | source)
XLA Modules:
  0.0 30.5 jit_solution(4345636094383551756)
XLA Ops:
  0.6 28.5 %picard.1 = (f32[2,3,1,384]{3,2,1,0:T(1,128)S(1)}, f32[3,32,768]{2,1,0:T(8,128)S(1)}) custom-call(s32[2,1,1024]{2,1,0:T(1,128)} %near_hbm.1, s32[1,256]{1,0:T(1,128)} %target_hbm.1, s32[1,256]{1,0:T(1,128)} %source_hbm.1, s32[1,32]{1,0:T(1,128)} %count_hbm.1, bf16[2,1,1152,1152]{3,2,1,0:T(8,128)(2,1)} %matrix_hbm.1, f32[2,3,1,384]{3,2,1,0:T(1,128)} %bitcast.4, ...), custom_call_target="tpu_custom_call" | custom-call | flops 2000000000 | bytes 8000000 | tf_op jit(solution)/shard_map/picard/pallas_call | solution.py:759
  29.1 0.6 %copy.13 = f32[2,1,3,384]{3,1,2,0:T(1,128)} copy(f32[2,1,3,384]{3,1,2,0:T(1,128)S(1)} %bitcast.3) | data formatting | bytes 18432
  29.7 0.7 %copy.14 = f32[3,32,768]{2,1,0:T(8,128)} copy(f32[3,32,768]{2,1,0:T(8,128)S(1)} %get-tuple-element.7) | data formatting | bytes 589824

commit v4 on v3

--- a/solution.py
+++ b/solution.py
@@ -444,15 +444,38 @@
             )
         )
 
-    def self_term(turn, k):
-        flat = jnp.concatenate(rows_of(state.at[1] if turn == 0 else dens1, k), axis=1)
-        rows = jnp.broadcast_to(flat, (16, flat.shape[1])).astype(BF16)
-        found = lax.dot_general(rows, matrix[k], MINOR, preferred_element_type=F32)
-        return [found[0:1, c * points : (c + 1) * points] for c in range(3)]
+    def self_terms(turn):
+        ref = state.at[1] if turn == 0 else dens1
+        size = matrix.shape[1]
+        half = LANES
+        whole = size - half
+        upper = lax.broadcasted_iota(jnp.int32, (16, size), 0) < ROWS
+        flat = [jnp.concatenate(rows_of(ref, k), axis=1) for k in range(cells)]
+        both = jnp.where(upper, flat[0], flat[1])
+        split = jnp.concatenate(
+            [jnp.where(upper[:, :half], both[:, whole:], 0.0), jnp.where(upper[:, :half], 0.0, both[:, whole:])],
+            axis=1,
+        ).astype(BF16)
+        front = both[:, :whole].astype(BF16)
+        tail = jnp.concatenate([matrix[k, :, pl.ds(whole, half)] for k in range(cells)], axis=1)
+        last = jnp.concatenate([matrix[k, pl.ds(whole, half), pl.ds(0, whole)] for k in range(cells)], axis=0)
+        tail = lax.dot_general(split, tail, MINOR, preferred_element_type=F32)
+        last = lax.dot_general(front, last, MINOR, preferred_element_type=F32)
+        out = []
+        for k in range(cells):
+            main = lax.dot_general(
+                front, matrix[k, pl.ds(0, whole), pl.ds(0, whole)], MINOR, preferred_element_type=F32
+            )
+            row = ROWS * k
+            found = jnp.concatenate(
+                [main[row : row + 1], last[row : row + 1, half * k : half * (k + 1)]], axis=1
+            ) + tail[row : row + 1]
+            out.append([found[:, c * points : (c + 1) * points] for c in range(3)])
+        return out
 
     for copy in inside[4:]:
         copy.wait()
-    velocity = [self_term(0, k) for k in range(cells)]
+    velocity = self_terms(0)
 
     slots = target_row.shape[1]
     slot = lax.broadcasted_iota(jnp.int32, (1, slots), 1)
@@ -693,7 +716,7 @@
         )
 
     make_packs(own_units, 3 * ROWS * len(units))
-    velocity = [self_term(1, k) for k in range(cells)]
+    velocity = self_terms(1)
 
     for copy in packs:
         copy.wait_recv()

time: 30.6 us -> 30.6 us (level)
  no operation moved by 1% of the time
where the time goes in v4:
time: 30.6 us; the launch traced here: 30.5 us
  Pallas kernels  28.5 us (93%)
  local copies, waits for them, and re-layouts  1.31 us (4%)
  between operations  0.64 us (2%)
    pallas_call x1, Pallas kernels, local(): pl.pallas_call(functools.partial(body, n_cell, n_wall), out_shape=(pltpu....  28.5 us
    unnamed x2, local copies, waits for them, and re-layouts  1.31 us

profile of v4, /device:TPU:1, one launch (start us, length us, event | category | flops | bytes accessed | tf_op | source)
XLA Modules:
  0.0 30.5 jit_solution(457407372576887501)
XLA Ops:
  0.6 28.5 %picard.1 = (f32[2,3,1,384]{3,2,1,0:T(1,128)S(1)}, f32[3,32,768]{2,1,0:T(8,128)S(1)}) custom-call(s32[2,1,1024]{2,1,0:T(1,128)} %near_hbm.1, s32[1,256]{1,0:T(1,128)} %target_hbm.1, s32[1,256]{1,0:T(1,128)} %source_hbm.1, s32[1,32]{1,0:T(1,128)} %count_hbm.1, bf16[2,1,1152,1152]{3,2,1,0:T(8,128)(2,1)} %matrix_hbm.1, f32[2,3,1,384]{3,2,1,0:T(1,128)} %bitcast.4, ...), custom_call_target="tpu_custom_call" | custom-call | flops 2000000000 | bytes 8000000 | tf_op jit(solution)/shard_map/picard/pallas_call | solution.py:782
  29.1 0.6 %copy.13 = f32[2,1,3,384]{3,1,2,0:T(1,128)} copy(f32[2,1,3,384]{3,1,2,0:T(1,128)S(1)} %bitcast.3) | data formatting | bytes 18432
  29.7 0.7 %copy.14 = f32[3,32,768]{2,1,0:T(8,128)} copy(f32[3,32,768]{2,1,0:T(8,128)S(1)} %get-tuple-element.7) | data formatting | bytes 589824
